TPU v7x, 128 devices: a whole 4x4x4 slice. The times are simulated.
128 devices in a mesh: rows: 16 (over z, y), serve: 8 (over x, core).
Axes of the slice: x: 4, y: 4, z: 4, core: 2. Of those that a mesh axis runs over, the one named last changes fastest.
Arguments:
- rows_small: float32 [131072, 32], P(('rows', 'serve')), may hold values from -6 to 6
- rows_mid: float32 [131072, 64], P(('rows', 'serve')), may hold values from -6 to 6
- rows_wide: float32 [131072, 128], P(('rows', 'serve')), may hold values from -6 to 6
- row_grads: float32 [3, 131072, 256], P(None, ('rows', 'serve'))
- proj_small: float32 [32, 256], replicated, may hold values from -1 to 1
- proj_mid: float32 [64, 256], replicated, may hold values from -0.75 to 0.75
- proj_wide: float32 [128, 256], replicated, may hold values from -0.5 to 0.5
- counts: int32 [3, 128], P(None, ('rows', 'serve')), may hold values from 512 to 1024, as said below
- owners: int32 [3, 131072, 1], P(None, ('rows', 'serve')), may hold values from 0 to 127; in each aligned block of 1024 rows (0 to 1023, 1024 to 2047, ..., all dimensions but the last counted through in order) at most 12 rows name the same one
Outputs:
- served: bfloat16 [196608, 768], P(('rows', 'serve'))
Inputs may be any that keep to these rules, and one draw needn't show every extreme that they name: `counts`: one device of each tier has all 1024 slots live. `owners`: among the 1024 slots of one device and tier at most 12 name one owner, and exactly 12 do for some owner.
All inputs are finite; a program needn't handle non-finite values.
Results may differ from a plain program's by a relative error of at most 0.001.
Values may be sent and summed in bfloat16 or wider, within the bound.
A program may use at most 64 MiB of HBM per device.

v0:
```python
import jax
import jax.numpy as jnp
from jax import lax
from jax.sharding import PartitionSpec as P

STEP_NORM = 16.0
ROW_RATE = 0.1


def refresh_factor(total):
    return STEP_NORM / jnp.sqrt(jnp.sum(total * total) + 1e-06)


def highest_dot(left, right):
    return jnp.dot(left, right, precision=lax.Precision.HIGHEST, preferred_element_type=jnp.float32)


def owner_slots(owner, valid, device_count, capacity):
    columns = jnp.arange(device_count, dtype=jnp.int32)
    matched = (owner[:, None] == columns[None, :]) & valid[:, None]
    hit_counts = matched.astype(jnp.int32)
    before = jnp.cumsum(hit_counts, axis=0) - hit_counts
    slot_index = jnp.sum(jnp.where(matched, before, 0), axis=1)
    return jnp.where(valid, owner * capacity + slot_index, device_count * capacity)


def place_rows(values, target, device_count, capacity):
    empty = jnp.zeros((device_count * capacity, values.shape[1]), values.dtype)
    return empty.at[target].set(values, mode="drop")


def sum_gradients(totals):
    return lax.psum((totals[0], totals[1], totals[2]), ("rows", "serve"))


def route_projected(buffer):
    return lax.all_to_all(buffer, ("rows", "serve"), split_axis=0, concat_axis=0, tiled=True)


def local(
    rows_small, rows_mid, rows_wide, row_grads, proj_small, proj_mid, proj_wide, counts, owners
):
    device_count = lax.axis_size("rows") * lax.axis_size("serve")
    slots_here = rows_small.shape[0]
    capacity = max(2, slots_here // device_count + slots_here // (2 * device_count))
    out_width = row_grads.shape[2]
    tables = (rows_small, rows_mid, rows_wide)
    projections = (proj_small, proj_mid, proj_wide)
    positions = jnp.arange(slots_here, dtype=jnp.int32)
    new_rows = []
    targets = []
    totals = []
    for tier_index in range(3):
        valid = positions < counts[tier_index, 0]
        gradients = jnp.where(valid[:, None], row_grads[tier_index], 0.0)
        totals.append(highest_dot(tables[tier_index].T, gradients))
        row_step = highest_dot(gradients, projections[tier_index].T)
        new_rows.append(tables[tier_index] - ROW_RATE * row_step)
        targets.append(owner_slots(owners[tier_index, :, 0], valid, device_count, capacity))
    summed = sum_gradients(totals)
    projected = []
    for tier_index in range(3):
        new_proj = projections[tier_index] - refresh_factor(summed[tier_index]) * summed[tier_index]
        projected.append(highest_dot(new_rows[tier_index], new_proj).astype(jnp.bfloat16))
    blocks = [
        place_rows(projected[tier_index], targets[tier_index], device_count, capacity)
        for tier_index in range(3)
    ]
    outgoing = jnp.concatenate(blocks, axis=1).reshape(device_count, capacity * 3 * out_width)
    moved = route_projected(outgoing)
    return moved.reshape(device_count * capacity, 3 * out_width)


def solution(mesh):
    return jax.shard_map(
        local,
        mesh=mesh,
        in_specs=(
            P(("rows", "serve"), None),
            P(("rows", "serve"), None),
            P(("rows", "serve"), None),
            P(None, ("rows", "serve"), None),
            P(),
            P(),
            P(),
            P(None, ("rows", "serve")),
            P(None, ("rows", "serve"), None),
        ),
        out_specs=P(("rows", "serve"), None),
        check_vma=False,
    )
```

profile of v0, /device:TPU:1, one launch (start us, length us, event | category | flops | bytes accessed | tf_op | source)
XLA Modules:
  0.0 280.6 jit_solution(69839678236443263)
XLA Ops:
  6.5 0.0 all-reduce.3.cloned.1.call-start
  6.6 1.5 fusion.67
  8.1 0.6 iota_compare_fusion.6
  8.7 0.7 iota_compare_fusion.7
  9.4 2.7 convolution_bitcast_fusion.1
  12.2 4.0 %convolution_bitcast_fusion = f32[128,256]{0,1:T(8,128)} fusion(f32[1024,128]{1,0:T(8,128)} %param.11, f32[3,1024,256]{2,1,0:T(8,128)} %param.12, pred[1024]{0:T(1024)(128)(4,1)S(1)} %iota_compare_fusion.6), kind=kOutput, calls=%fused_computation.13 | convolution fusion | flops 402915328 | bytes 1704960 | tf_op jit(solution)/shard_map/dot_general | solution.py:15
  16.1 0.0 all-reduce.3.cloned.1.call-update
  16.2 0.6 iota_compare_fusion.8
  16.8 1.2 fusion.55
  17.9 1.2 fusion.53
  19.2 0.7 fusion.54
  19.9 0.0 copy-done.9
  20.0 0.8 convolution_bitcast_fusion.2
  20.8 70.0 %psum.21 = f32[32,256]{1,0:T(8,128)S(1)} all-reduce(f32[32,256]{1,0:T(8,128)S(1)} %convolution_bitcast_fusion.2), channel_id=1, replica_groups=mesh['rows'=16,'serve'=8] {'rows','serve'}, use_global_device_ids=true, to_apply=%region_3.4 | all-reduce | flops 8192 | bytes 65536 | tf_op jit(solution)/shard_map/psum | solution.py:33
  90.8 0.6 multiply_reduce_fusion.2
  92.1 0.7 copy.30
  92.8 0.7 copy.32
  93.5 0.7 copy.28
  94.3 0.0 copy-done.14
  94.3 1.2 fusion.2
  95.5 2.2 fusion.1
  97.7 1.2 fusion.19
  98.9 0.0 copy-start.2
  98.9 0.8 copy-done.2
  99.7 0.6 slice_bitcast_fusion.2
  100.3 1.3 reduce-window.21
  101.6 0.7 slice.61
  102.3 1.1 broadcast_add_fusion.2
  103.4 0.9 copy.29
  104.3 1.2 fusion.9
  105.5 0.8 copy-done.3
  106.2 0.6 slice_bitcast_fusion
  106.8 1.3 reduce-window.29
  108.1 0.7 slice.65
  108.8 1.1 broadcast_add_fusion
  109.9 0.9 copy.33
  110.8 1.2 fusion.11
  112.0 0.8 copy-done.1
  112.8 1.1 broadcast_add_fusion.1
  113.9 0.9 copy.31
  114.8 3.0 %fusion = f32[1024,128]{1,0:T(8,128)} fusion(f32[1024,128]{1,0:T(8,128)} %param.11, f32[128,256]{1,0:T(8,128)} %param.15, f32[3,1024,256]{2,1,0:T(8,128)S(1)} %copy-done, pred[1024]{0:T(1024)(128)(4,1)} %copy-done.15), kind=kOutput, calls=%fused_computation.8 | convolution fusion | flops 403177472 | bytes 2229248 | tf_op jit(solution)/shard_map/dot_general | solution.py:15
  117.8 1.9 convolution_convert_fusion.2
  119.7 1.6 fusion.8
  121.2 1.6 fusion.4
  122.8 1.6 fusion.6
  124.4 1.9 compare_select_fusion.2
  126.3 1.0 copy.34
  127.3 5.4 %scatter_custom_fusion = bf16[1536,256]{1,0:T(8,128)(2,1)S(1)} fusion(s32[1024]{0:T(1024)S(1)} %bitcast.98, bf16[1024,256]{1,0:T(8,128)(2,1)S(1)} %convolution_convert_fusion.2, bf16[]{:T(256)} %constant.9.clone.1), kind=kCustom, calls=%fused_computation.62 | custom fusion | bytes 786434 | tf_op jit(solution)/shard_map/scatter | solution.py:29
  132.7 29.7 %all-reduce.3.cloned.1.call-done = (f32[128,256]{0,1:T(8,128)}, f32[64,256]{1,0:T(8,128)}) async-done(((f32[128,256]{0,1:T(8,128)}, f32[64,256]{1,0:T(8,128)}), (f32[128,256]{0,1:T(8,128)}, f32[64,256]{1,0:T(8,128)})) %all-reduce.3.cloned.1.call-update) | async-done | bytes 196624 | tf_op jit(solution)/shard_map/psum | solution.py:33
  162.4 1.5 multiply_reduce_fusion.1
  164.6 1.5 multiply_reduce_fusion
  166.8 1.9 convolution_convert_fusion.1
  168.7 5.9 %scatter_custom_fusion.1 = bf16[1536,256]{1,0:T(8,128)(2,1)} fusion(s32[1024]{0:T(1024)S(1)} %bitcast.97, bf16[1024,256]{1,0:T(8,128)(2,1)S(1)} %convolution_convert_fusion.1, bf16[]{:T(256)} %constant.9.clone.1), kind=kCustom, calls=%fused_computation.60 | custom fusion | bytes 786434 | tf_op jit(solution)/shard_map/scatter | solution.py:29
  174.5 1.9 convolution_convert_fusion
  176.4 5.9 %scatter_custom_fusion.2 = bf16[1536,256]{1,0:T(8,128)(2,1)} fusion(s32[1024]{0:T(1024)S(1)} %bitcast.96, bf16[1024,256]{1,0:T(8,128)(2,1)S(1)} %convolution_convert_fusion, bf16[]{:T(256)} %constant.9.clone.1), kind=kCustom, calls=%fused_computation.58 | custom fusion | bytes 786434 | tf_op jit(solution)/shard_map/scatter | solution.py:29
  182.3 1.5 pad_maximum_fusion
  183.8 6.3 %all_to_all.8 = bf16[128,1,9216]{2,1,0:T(2,128)(2,1)} reshape(bf16[1536,768]{1,0:T(8,128)(2,1)S(1)} %pad_maximum_fusion) | data formatting | bytes 4718592 | tf_op jit(solution)/shard_map/all_to_all | solution.py:37
  190.2 0.5 broadcast.201
  190.7 14.8 %reduce.1 = bf16[128,9216]{1,0:T(8,128)(2,1)S(1)} reduce(bf16[128,1,9216]{2,1,0:T(2,128)(2,1)} %all_to_all.8, bf16[]{:T(256)} %broadcast.201), dimensions={1}, to_apply=%all_to_all.8.reduce_sub_computation | reduce | bytes 4718594 | tf_op jit(solution)/shard_map/all_to_all | solution.py:37
  205.5 3.0 %reshape.232 = bf16[128,2,4608]{2,1,0:T(2,128)(2,1)} reshape(bf16[128,9216]{1,0:T(8,128)(2,1)S(1)} %reduce.1) | data formatting | bytes 4718592
  208.4 39.9 %all_to_all.10 = bf16[128,2,4608]{2,1,0:T(2,128)(2,1)S(1)} all-to-all(bf16[128,2,4608]{2,1,0:T(2,128)(2,1)} %reshape.232), channel_id=1, replica_groups=mesh['rows'=16,'serve'=8] {'rows','serve'}, dimensions={0} | all-to-all | bytes 4718592 | tf_op jit(solution)/shard_map/all_to_all | solution.py:37
  248.3 6.7 %reshape.233 = bf16[128,1,9216]{2,1,0:T(2,128)(2,1)} reshape(bf16[128,2,4608]{2,1,0:T(2,128)(2,1)S(1)} %all_to_all.10) | data formatting | bytes 4718592
  255.1 14.1 %reduce = bf16[128,9216]{1,0:T(8,128)(2,1)S(1)} reduce(bf16[128,1,9216]{2,1,0:T(2,128)(2,1)} %reshape.233, bf16[]{:T(256)} %constant.30), dimensions={1}, to_apply=%all_to_all.7.reduce_sub_computation | reduce | bytes 4718594 | tf_op jit(solution)/shard_map/all_to_all | solution.py:37
  269.2 4.5 %reshape.200 = bf16[1536,768]{1,0:T(8,128)(2,1)} reshape(bf16[128,9216]{1,0:T(8,128)(2,1)S(1)} %reduce) | data formatting | bytes 4718592 | tf_op jit(solution)/shard_map/reshape | solution.py:71
  (34 shorter events, 0.1 us)
Async XLA Ops:
  6.5 13.4 %copy-start = (f32[3,1024,256]{2,1,0:T(8,128)S(1)}, f32[3,1024,256]{2,1,0:T(8,128)}, u32[]{:S(2)}) copy-start(f32[3,1024,256]{2,1,0:T(8,128)} %param.12) | copy-start | bytes 9437188
  6.5 13.3 %copy-start.9 = (s32[3,1024,1]{1,2,0:T(1,128)S(1)}, s32[3,1024,1]{1,2,0:T(1,128)}, u32[]{:S(2)}) copy-start(s32[3,1024,1]{1,2,0:T(1,128)} %param.17) | copy-start | bytes 36868
  6.5 13.4 %copy-start.5 = (f32[1024,32]{0,1:T(8,128)S(1)}, f32[1024,32]{0,1:T(8,128)}, u32[]{:S(2)}) copy-start(f32[1024,32]{0,1:T(8,128)} %param.9) | copy-start | bytes 393220
  6.5 87.7 %copy-start.8 = (f32[32,256]{1,0:T(8,128)S(1)}, f32[32,256]{1,0:T(8,128)}, u32[]{:S(2)}) copy-start(f32[32,256]{1,0:T(8,128)} %param.13) | copy-start | bytes 98308
  6.5 155.9 %all-reduce.3.cloned.1.call-start = ((), (), s32[]{:S(2)}) async-start(), calls=%async_computation.1 | async-start | bytes 393216 | tf_op jit(solution)/shard_map/psum | solution.py:33
  8.7 11.2 %copy-start.15 = (pred[1024]{0:T(1024)(128)(4,1)}, pred[1024]{0:T(1024)(128)(4,1)S(1)}, u32[]{:S(2)}) copy-start(pred[1024]{0:T(1024)(128)(4,1)S(1)} %iota_compare_fusion.6) | copy-start | bytes 3076
  9.4 10.5 %copy-start.16 = (pred[1024]{0:T(1024)(128)(4,1)}, pred[1024]{0:T(1024)(128)(4,1)S(1)}, u32[]{:S(2)}) copy-start(pred[1024]{0:T(1024)(128)(4,1)S(1)} %iota_compare_fusion.7) | copy-start | bytes 3076
  16.7 77.5 %copy-start.17 = (pred[1024]{0:T(1024)(128)(4,1)}, pred[1024]{0:T(1024)(128)(4,1)S(1)}, u32[]{:S(2)}) copy-start(pred[1024]{0:T(1024)(128)(4,1)S(1)} %iota_compare_fusion.8) | copy-start | bytes 3076
  19.9 74.3 %copy-start.11 = (s32[1,1024,1]{1,2,0:T(1,128)}, s32[1,1024,1]{1,2,0:T(1,128)S(1)}, u32[]{:S(2)}) copy-start(s32[1,1024,1]{1,2,0:T(1,128)S(1)} %get-tuple-element.12) | copy-start | bytes 12292
  19.9 74.3 %copy-start.13 = (s32[1,1024,1]{1,2,0:T(1,128)}, s32[1,1024,1]{1,2,0:T(1,128)S(1)}, u32[]{:S(2)}) copy-start(s32[1,1024,1]{1,2,0:T(1,128)S(1)} %get-tuple-element.11) | copy-start | bytes 12292
  20.0 74.3 %copy-start.14 = (s32[1,1024,1]{1,2,0:T(1,128)}, s32[1,1024,1]{1,2,0:T(1,128)S(1)}, u32[]{:S(2)}) copy-start(s32[1,1024,1]{1,2,0:T(1,128)S(1)} %get-tuple-element.10) | copy-start | bytes 12292
  90.8 3.5 %copy-start.6 = (f32[32,256]{1,0:T(8,128)}, f32[32,256]{1,0:T(8,128)S(1)}, u32[]{:S(2)}) copy-start(f32[32,256]{1,0:T(8,128)S(1)} %psum.21) | copy-start | bytes 98308
  98.9 0.8 copy-start.2
  105.5 0.8 copy-start.3
  112.0 0.8 copy-start.1
  112.8 10.0 %copy-start.12 = (s32[1,1024,1]{1,2,0:T(1,128)S(1)}, s32[1,1024,1]{1,2,0:T(1,128)}, u32[]{:S(2)}) copy-start(s32[1,1024,1]{1,2,0:T(1,128)} %copy-done.11) | copy-start | bytes 12292
  112.8 11.5 %copy-start.10 = (s32[3,1024,1]{1,2,0:T(1,128)S(1)}, s32[3,1024,1]{1,2,0:T(1,128)}, u32[]{:S(2)}) copy-start(s32[3,1024,1]{1,2,0:T(1,128)} %param.17) | copy-start | bytes 36868
  117.8 49.0 %copy-start.7 = (f32[64,256]{1,0:T(8,128)S(1)}, f32[64,256]{1,0:T(8,128)}, u32[]{:S(2)}) copy-start(f32[64,256]{1,0:T(8,128)} %param.14) | copy-start | bytes 196612
  117.8 56.8 %copy-start.4 = (f32[1024,128]{1,0:T(8,128)S(1)}, f32[1024,128]{1,0:T(8,128)}, u32[]{:S(2)}) copy-start(f32[1024,128]{1,0:T(8,128)} %fusion) | copy-start | bytes 1572868
Sparse Core Ops, SparseCore 0:
  16.3 146.0 all-reduce.2
where the time goes:
time: 282 us; the launch traced here: 281 us
  blocking collectives  110 us (39%)
  other arithmetic  55 us (20%)
  local copies, waits for them, and re-layouts  50.5 us (18%)
  waiting for transfers between devices  29.8 us (11%)
  matrix products  19.5 us (7%)
  between operations  15.8 us (6%)
    psum x1, blocking collectives, sum_gradients(): return lax.psum((totals[0], totals[1], totals[2]), ('rows', 'serve'))  70 us
    all_to_all x1, blocking collectives, route_projected(): lax.all_to_all(buffer, ('rows', 'serve'), split_axis=0, concat_axis=0, ti...  39.9 us
    psum x1, waiting for transfers between devices, sum_gradients(): return lax.psum((totals[0], totals[1], totals[2]), ('rows', 'serve'))  29.7 us
    all_to_all x2, other arithmetic, route_projected(): lax.all_to_all(buffer, ('rows', 'serve'), split_axis=0, concat_axis=0, ti...  28.9 us
    dot_general x9, matrix products, highest_dot(): jnp.dot(left, right, precision=lax.Precision.HIGHEST, preferred_element_t...  19.5 us
    scatter x3, local copies, waits for them, and re-layouts, place_rows(): return empty.at[target].set(values, mode='drop')  17.1 us
    unnamed x39, local copies, waits for them, and re-layouts  13.1 us
    another operation x9, other arithmetic  9.38 us
  transfers between devices with their start and end apart: 1, of which 1 were waited for; matrix products, arithmetic and copies ran while one was open for 15% of the time, Pallas kernels for 0%

commit v1 on v0

v1 whole, which is shorter than its diff:
```python
import functools

import jax
import jax.numpy as jnp
from jax import lax
from jax.experimental import pallas as pl
from jax.experimental.pallas import tpu as pltpu
from jax.sharding import PartitionSpec as P

STEP_NORM = 16.0
ROW_RATE = 0.1
MESH = pl.DeviceIdType.MESH
N_ROWS = 16
N_SERVE = 8
DEVS = 128
CAP = 12
SLOTS = DEVS * CAP
ROWS = 1024
D = 256
LANES = 128
BLOCK = 2 * CAP
PAIRS_STEP = 8
CHUNK = PAIRS_STEP * BLOCK
F32 = jnp.float32
BF16 = jnp.bfloat16


def split(x):
    high = x.astype(BF16)
    low = (x - high.astype(F32)).astype(BF16)
    return high, low


def dot(a, b):
    return lax.dot_general(a, b, (((1,), (0,)), ((), ())), preferred_element_type=F32)


def dot_nt(a, b):
    return lax.dot_general(a, b, (((1,), (1,)), ((), ())), preferred_element_type=F32)


def place_of(p):
    return (p // N_SERVE, p % N_SERVE)


def peer_of(me, r):
    z = (me // 32 + r // 32) % 4
    y = (me // 8 + r // 8) % 4
    x = (me // 2 + r // 2) % 4
    return z * 32 + y * 8 + x * 2 + (me + r) % 2


def half_turn(x):
    return pltpu.roll(x, 4, 1)


def front_kernel(
    small_hbm, mid_hbm, wide_hbm, grads_hbm, ps_hbm, pm_hbm, pw_hbm, counts_ref, owners_hbm,
    recv_hbm, weights_ref,
    small, mid, wide, grads, ps, pm, pw, owners,
    placed_w, placed_m, placed_s, targets, send, totals, stage1, sum1, stage2, full,
    in_sem, send_sem, recv_sem, red_send, red_recv, own_sem,
):
    rows_at = lax.axis_index("rows")
    serve_at = lax.axis_index("serve")
    me = rows_at * N_SERVE + serve_at

    sources = (owners_hbm, small_hbm, mid_hbm, wide_hbm, ps_hbm, pm_hbm, pw_hbm)
    holders = (owners, small, mid, wide, ps, pm, pw)
    loads = [pltpu.make_async_copy(s, h, in_sem.at[i]) for i, (s, h) in enumerate(zip(sources, holders))]
    grad_loads = [
        pltpu.make_async_copy(grads_hbm.at[t], grads.at[t], in_sem.at[len(loads) + t]) for t in range(3)
    ]
    for load in loads:
        load.start()
    for t in (2, 1, 0):
        grad_loads[t].start()

    barrier = pltpu.get_barrier_semaphore()

    def greet(j, carry):
        pl.semaphore_signal(barrier, inc=1, device_id=place_of(peer_of(me, j)), device_id_type=MESH)
        return carry

    lax.fori_loop(1, DEVS, greet, 0)

    loads[0].wait()
    lane = lax.broadcasted_iota(jnp.int32, (1, ROWS), 1)
    named = lax.broadcasted_iota(jnp.int32, (DEVS, ROWS), 0)
    hits = []
    for t in range(3):
        live = lane < counts_ref[0, t]
        owner = jnp.where(live, owners[t], -1)
        hits.append(jnp.where(named == owner, 1.0, 0.0).astype(BF16))
    hit = jnp.concatenate(hits, axis=0)
    ahead = lax.broadcasted_iota(jnp.int32, (256, 256), 0) < lax.broadcasted_iota(jnp.int32, (256, 256), 1)
    ahead = jnp.where(ahead, 1.0, 0.0).astype(BF16)
    carry = jnp.zeros((3 * DEVS, 1), F32)
    ranks = []
    for c in range(ROWS // 256):
        part = hit[:, c * 256:(c + 1) * 256]
        before = dot(part, ahead) + carry
        mine = part.astype(F32)
        carry = before[:, 255:256] + mine[:, 255:256]
        ranks.append(jnp.sum((before * mine).reshape(3, DEVS, 256), axis=1))
    rank = jnp.concatenate(ranks, axis=1).astype(jnp.int32)
    for t in range(3):
        owner = owners[t]
        turn = jnp.where(owner % 2 == me % 2, 0, jnp.where(owner % 2 == 0, 8, 4))
        slot = rank[t:t + 1] + turn
        slot = jnp.where(slot >= CAP, slot - CAP, slot)
        live = lane < counts_ref[0, t]
        targets[t] = jnp.where(live, owner * CAP + slot, -1)

    for load in loads[1:]:
        load.wait()
    wide_t = wide[...].T
    both_t = jnp.concatenate([mid[...], small[...], jnp.zeros((32, ROWS), F32)], axis=0)
    both = both_t.T
    column = lax.broadcasted_iota(jnp.int32, (ROWS, LANES), 1)
    zeros = lambda n: jnp.zeros((n, D), F32)
    tiers = (
        (2, wide_t, wide[...], pw[...], placed_w),
        (1, mid[...], jnp.where(column < 64, both, 0.0),
         jnp.concatenate([pm[...], zeros(64)], axis=0), placed_m),
        (0, small[...], jnp.where(column >= 64, both, 0.0),
         jnp.concatenate([zeros(64), ps[...], zeros(32)], axis=0), placed_s),
    )
    at = 0
    row = lax.broadcasted_iota(jnp.int32, (ROWS, D), 0)
    for t, table_t, table, projection, placed in tiers:
        grad_loads[t].wait()
        masked = jnp.where(row < counts_ref[0, t], grads[t], 0.0)
        g_high, g_low = split(masked)
        e_high, e_low = split(table_t)
        total = dot(e_high, g_high) + (dot(e_low, g_high) + dot(e_high, g_low))
        width = table_t.shape[0]
        totals[at:at + width, :] = total[:, :LANES]
        totals[at + width:at + 2 * width, :] = total[:, LANES:]
        at += 2 * width
        p_high, p_low = split(projection)
        step = dot_nt(g_high, p_high) + (dot_nt(g_low, p_high) + dot_nt(g_high, p_low))
        moved = table - ROW_RATE * step
        high, low = split(moved)
        placed[:, :LANES] = high
        placed[:, LANES:] = low
    totals[at:, :] = jnp.zeros((512 - at, LANES), F32)

    slot_row = lax.broadcasted_iota(jnp.int32, (CHUNK, ROWS), 0)
    lower = lax.broadcasted_iota(jnp.int32, (PAIRS_STEP, 8, LANES), 1) < 4

    def place(c, carry):
        base = c * CHUNK

        def chosen(t):
            return jnp.where(slot_row == targets[t] - base, 1.0, 0.0).astype(BF16)

        got_a = dot(chosen(2), placed_w[...])
        got_b = dot(chosen(1), placed_m[...]) + dot(chosen(0), placed_s[...])
        a = (got_a[:, :LANES] + got_a[:, LANES:]).reshape(PAIRS_STEP, BLOCK, LANES)
        b = (got_b[:, :LANES] + got_b[:, LANES:]).reshape(PAIRS_STEP, BLOCK, LANES)
        at = pl.ds(c * PAIRS_STEP, PAIRS_STEP)
        a_half, b_half = a[:, 8:16], b[:, 8:16]
        send[at, 0, 0:8] = a[:, 0:8]
        send[at, 0, 8:16] = b[:, 0:8]
        send[at, 0, 16:24] = jnp.where(lower, a_half, half_turn(b_half))
        send[at, 1, 0:8] = a[:, 16:24]
        send[at, 1, 8:16] = b[:, 16:24]
        send[at, 1, 16:24] = jnp.where(lower, half_turn(a_half), b_half)
        return carry

    lax.fori_loop(0, SLOTS // CHUNK, place, 0)

    pl.semaphore_wait(barrier, DEVS - 1)

    def route(j, carry):
        p = peer_of(me, (j * 37) % DEVS)
        pltpu.make_async_remote_copy(
            send.at[p // 2, p % 2], recv_hbm.at[me], send_sem, recv_sem,
            device_id=place_of(p), device_id_type=MESH,
        ).start()
        return carry

    def scatter_rows(j, carry):
        p = (rows_at + j) % N_ROWS
        pltpu.make_async_remote_copy(
            totals.at[pl.ds(pl.multiple_of(p * 32, 32), 32)], stage1.at[rows_at], red_send.at[0], red_recv.at[0],
            device_id=(p, serve_at), device_id_type=MESH,
        ).start()
        return carry

    def swap_serve(j, carry):
        p = (serve_at + j) % N_SERVE
        pltpu.make_async_remote_copy(
            sum1, stage2.at[serve_at], red_send.at[1], red_recv.at[1],
            device_id=(rows_at, p), device_id_type=MESH,
        ).start()
        return carry

    def gather_rows(j, carry):
        p = (rows_at + j) % N_ROWS
        pltpu.make_async_remote_copy(
            full.at[rows_at], full.at[rows_at], red_send.at[2], red_recv.at[2],
            device_id=(p, serve_at), device_id_type=MESH,
        ).start()
        return carry

    def all_of(ref, n, sem):
        pltpu.make_async_copy(ref.at[pl.ds(0, n)], ref.at[pl.ds(0, n)], sem).wait()

    lax.fori_loop(1, N_ROWS, scatter_rows, 0)
    own = pltpu.make_async_copy(send.at[me // 2, me % 2], recv_hbm.at[me], own_sem)
    own.start()
    lax.fori_loop(1, 48, route, 0)
    stage1[rows_at] = totals[pl.ds(pl.multiple_of(rows_at * 32, 32), 32), :]
    all_of(stage1, N_ROWS - 1, red_recv.at[0])
    sum1[...] = jnp.sum(stage1[...], axis=0)
    lax.fori_loop(1, N_SERVE, swap_serve, 0)
    lax.fori_loop(48, 88, route, 0)
    stage2[serve_at] = sum1[...]
    all_of(stage2, N_SERVE - 1, red_recv.at[1])
    full[rows_at] = jnp.sum(stage2[...], axis=0)
    lax.fori_loop(1, N_ROWS, gather_rows, 0)
    lax.fori_loop(88, DEVS, route, 0)
    all_of(full, N_ROWS - 1, red_recv.at[2])

    summed = full[...].reshape(512, LANES)
    at = 0
    fresh = []
    for projection in (pw[...], pm[...], ps[...]):
        width = projection.shape[0]
        total = jnp.concatenate([summed[at:at + width], summed[at + width:at + 2 * width]], axis=1)
        at += 2 * width
        size = jnp.sum(total * total, axis=(0, 1), keepdims=True)
        fresh.append(projection - (STEP_NORM / jnp.sqrt(size + 1e-06)) * total)
    columns = (
        jnp.concatenate([zeros(64), fresh[2], zeros(32)], axis=0),
        jnp.concatenate([fresh[1], zeros(64)], axis=0),
        fresh[0],
    )
    for t in range(3):
        high, low = split(columns[t])
        weights_ref[0:128, t * D:(t + 1) * D] = high
        weights_ref[128:256, t * D:(t + 1) * D] = high
        weights_ref[256:384, t * D:(t + 1) * D] = low

    own.wait()
    all_of(recv_hbm, DEVS - 1, recv_sem)
    pltpu.make_async_copy(recv_hbm.at[pl.ds(0, DEVS - 1)], recv_hbm.at[pl.ds(0, DEVS - 1)], send_sem).wait()
    all_of(stage1, N_ROWS - 1, red_send.at[0])
    all_of(stage2, N_SERVE - 1, red_send.at[1])
    all_of(full, N_ROWS - 1, red_send.at[2])


def project_kernel(recv_ref, weights_ref, out_ref):
    pairs = recv_ref.shape[0] // 2
    got = recv_ref[...].reshape(pairs, 2, BLOCK, LANES)
    even, odd = got[:, 0], got[:, 1]
    lower = lax.broadcasted_iota(jnp.int32, (pairs, 8, LANES), 1) < 4
    even_half, odd_half = even[:, 16:24], odd[:, 16:24]
    a_half = jnp.where(lower, even_half, half_turn(odd_half))
    b_half = jnp.where(lower, half_turn(even_half), odd_half)
    a = jnp.concatenate([even[:, 0:8], a_half, odd[:, 0:8]], axis=1).reshape(pairs * BLOCK, LANES)
    b = jnp.concatenate([even[:, 8:16], b_half, odd[:, 8:16]], axis=1).reshape(pairs * BLOCK, LANES)
    for rows, first, last in ((b, 0, 2 * D), (a, 2 * D, 3 * D)):
        high, low = split(rows)
        both = jnp.concatenate([high, low, high], axis=1)
        out_ref[:, first:last] = dot(both, weights_ref[:, first:last]).astype(BF16)


def local(rows_small, rows_mid, rows_wide, row_grads, proj_small, proj_mid, proj_wide, counts, owners):
    hbm = pl.BlockSpec(memory_space=pl.ANY)
    vmem = pl.BlockSpec(memory_space=pltpu.VMEM)
    recv, weights = pl.pallas_call(
        front_kernel,
        out_shape=(
            jax.ShapeDtypeStruct((DEVS, BLOCK, LANES), F32),
            jax.ShapeDtypeStruct((384, 3 * D), BF16),
        ),
        in_specs=[hbm] * 7 + [pl.BlockSpec(memory_space=pltpu.SMEM), hbm],
        out_specs=(hbm, vmem),
        scratch_shapes=[
            pltpu.VMEM((32, ROWS), F32),
            pltpu.VMEM((64, ROWS), F32),
            pltpu.VMEM((ROWS, LANES), F32),
            pltpu.VMEM((3, ROWS, D), F32),
            pltpu.VMEM((32, D), F32),
            pltpu.VMEM((64, D), F32),
            pltpu.VMEM((128, D), F32),
            pltpu.VMEM((3, 1, ROWS), jnp.int32),
            pltpu.VMEM((ROWS, 2 * LANES), BF16),
            pltpu.VMEM((ROWS, 2 * LANES), BF16),
            pltpu.VMEM((ROWS, 2 * LANES), BF16),
            pltpu.VMEM((3, 1, ROWS), jnp.int32),
            pltpu.VMEM((DEVS // 2, 2, BLOCK, LANES), F32),
            pltpu.VMEM((512, LANES), F32),
            pltpu.VMEM((N_ROWS, 32, LANES), F32),
            pltpu.VMEM((32, LANES), F32),
            pltpu.VMEM((N_SERVE, 32, LANES), F32),
            pltpu.VMEM((N_ROWS, 32, LANES), F32),
            pltpu.SemaphoreType.DMA((10,)),
            pltpu.SemaphoreType.DMA,
            pltpu.SemaphoreType.DMA,
            pltpu.SemaphoreType.DMA((3,)),
            pltpu.SemaphoreType.DMA((3,)),
            pltpu.SemaphoreType.DMA,
        ],
        compiler_params=pltpu.CompilerParams(
            collective_id=0, has_side_effects=True, vmem_limit_bytes=48 << 20
        ),
        cost_estimate=pl.CostEstimate(flops=4_000_000_000, bytes_accessed=8_000_000, transcendentals=0),
        name="step_and_route",
    )(
        rows_small.T, rows_mid.T, rows_wide, row_grads, proj_small, proj_mid, proj_wide,
        counts.T, jnp.transpose(owners, (0, 2, 1)),
    )
    step = 16
    return pl.pallas_call(
        project_kernel,
        grid=(DEVS // step,),
        out_shape=jax.ShapeDtypeStruct((SLOTS, 3 * D), BF16),
        in_specs=[
            pl.BlockSpec((step, BLOCK, LANES), lambda i: (i, 0, 0)),
            pl.BlockSpec((384, 3 * D), lambda i: (0, 0)),
        ],
        out_specs=pl.BlockSpec((step * CAP, 3 * D), lambda i: (i, 0)),
        compiler_params=pltpu.CompilerParams(vmem_limit_bytes=32 << 20),
        cost_estimate=pl.CostEstimate(flops=1_000_000_000, bytes_accessed=5_000_000, transcendentals=0),
        name="project",
    )(recv, weights)


def solution(mesh):
    return jax.shard_map(
        local,
        mesh=mesh,
        in_specs=(
            P(("rows", "serve"), None),
            P(("rows", "serve"), None),
            P(("rows", "serve"), None),
            P(None, ("rows", "serve"), None),
            P(),
            P(),
            P(),
            P(None, ("rows", "serve")),
            P(None, ("rows", "serve"), None),
        ),
        out_specs=P(("rows", "serve"), None),
        check_vma=False,
    )
```

time: 282 us -> 61.2 us (0.22)
  blocking collectives: 110 us -> 0 us
  other arithmetic: 55 us -> 0 us
  Pallas kernels: 0 us -> 54.1 us
  local copies, waits for them, and re-layouts: 50.5 us -> 6.76 us
  waiting for transfers between devices: 29.8 us -> 0 us
  matrix products: 19.5 us -> 0 us
  between operations: 15.8 us -> 0.02 us
    psum x1 -> x0, blocking collectives: 70 us -> none  [sum_gradients(): return lax.psum((totals[0], totals[1], totals[2]), ('rows', 'serve'))]
    pallas_call x0 -> x2, Pallas kernels: none -> 54.1 us  [the longest x1 49.6 us: local(): pl.pallas_call(front_kernel, out_shape=(jax.ShapeDtypeStruct((DEVS, BLOCK...]
    all_to_all x1 -> x0, blocking collectives: 39.9 us -> none  [route_projected(): lax.all_to_all(buffer, ('rows', 'serve'), split_axis=0, concat_axis=0, ti...]
    psum x1 -> x0, waiting for transfers between devices: 29.7 us -> none  [sum_gradients(): return lax.psum((totals[0], totals[1], totals[2]), ('rows', 'serve'))]
    all_to_all x2 -> x0, other arithmetic: 28.9 us -> none  [route_projected(): lax.all_to_all(buffer, ('rows', 'serve'), split_axis=0, concat_axis=0, ti...]
    dot_general x9 -> x0, matrix products: 19.5 us -> none  [highest_dot(): jnp.dot(left, right, precision=lax.Precision.HIGHEST, preferred_element_t...]
    scatter x3 -> x0, local copies, waits for them, and re-layouts: 17.1 us -> none  [place_rows(): return empty.at[target].set(values, mode='drop')]
    another operation x9 -> x0, other arithmetic: 9.38 us -> none
  transfers between devices with their start and end apart: 1 -> 0, of which waited for: 1 -> 0; matrix products, arithmetic and copies ran while one was open for 15% -> 0% of each run, Pallas kernels for 0% -> 0%
where the time goes in v1:
time: 61.2 us; the launch traced here: 60.8 us
  Pallas kernels  54.1 us (88%)
  local copies, waits for them, and re-layouts  6.76 us (11%)
    pallas_call x1, Pallas kernels, local(): pl.pallas_call(front_kernel, out_shape=(jax.ShapeDtypeStruct((DEVS, BLOCK...  49.6 us
    unnamed x16, local copies, waits for them, and re-layouts  6.76 us
    pallas_call x1, Pallas kernels, local(): pl.pallas_call(project_kernel, grid=(DEVS // step,), out_shape=jax.ShapeD...  4.47 us

profile of v1, /device:TPU:1, one launch (start us, length us, event | category | flops | bytes accessed | tf_op | source)
XLA Modules:
  0.0 60.8 jit_solution(10226394779642745251)
XLA Ops:
  0.0 0.0 copy-start
  0.0 1.0 %copy-done = f32[1024,128]{1,0:T(8,128)S(1)} copy-done((f32[1024,128]{1,0:T(8,128)S(1)}, f32[1024,128]{1,0:T(8,128)}, u32[]{:S(2)}) %copy-start) | copy-done | bytes 524312
  1.0 0.0 copy-start.1
  1.0 0.9 %copy-done.1 = f32[1024,64]{0,1:T(8,128)S(1)} copy-done((f32[1024,64]{0,1:T(8,128)S(1)}, f32[1024,64]{0,1:T(8,128)}, u32[]{:S(2)}) %copy-start.1) | copy-done | bytes 262168
  2.0 0.0 copy-start.2
  2.0 0.9 %copy-done.2 = f32[1024,32]{0,1:T(8,128)S(1)} copy-done((f32[1024,32]{0,1:T(8,128)S(1)}, f32[1024,32]{0,1:T(8,128)}, u32[]{:S(2)}) %copy-start.2) | copy-done | bytes 131096
  2.9 0.0 copy-start.3
  2.9 0.9 %copy-done.3 = f32[128,256]{1,0:T(8,128)S(1)} copy-done((f32[128,256]{1,0:T(8,128)S(1)}, f32[128,256]{1,0:T(8,128)}, u32[]{:S(2)}) %copy-start.3) | copy-done | bytes 131096
  3.8 0.0 copy-start.4
  3.8 0.8 %copy-done.4 = f32[64,256]{1,0:T(8,128)S(1)} copy-done((f32[64,256]{1,0:T(8,128)S(1)}, f32[64,256]{1,0:T(8,128)}, u32[]{:S(2)}) %copy-start.4) | copy-done | bytes 65560
  4.6 0.0 copy-start.5
  4.6 0.8 %copy-done.5 = f32[32,256]{1,0:T(8,128)S(1)} copy-done((f32[32,256]{1,0:T(8,128)S(1)}, f32[32,256]{1,0:T(8,128)}, u32[]{:S(2)}) %copy-start.5) | copy-done | bytes 32792
  5.4 0.0 copy-start.6
  5.4 0.7 %copy-done.6 = s32[3,1024,1]{1,2,0:T(1,128)S(1)} copy-done((s32[3,1024,1]{1,2,0:T(1,128)S(1)}, s32[3,1024,1]{1,2,0:T(1,128)}, u32[]{:S(2)}) %copy-start.6) | copy-done | bytes 12312
  6.1 0.0 copy-start.7
  6.1 0.7 %copy-done.7 = s32[3,1]{0,1:T(1,128)S(1)} copy-done((s32[3,1]{0,1:T(1,128)S(1)}, s32[3,1]{0,1:T(1,128)}, u32[]{:S(2)}) %copy-start.7) | copy-done | bytes 36
  6.8 49.6 %step_and_route.1 = (f32[128,24,128]{2,1,0:T(8,128)S(1)}, bf16[384,768]{1,0:T(8,128)(2,1)S(1)}) custom-call(f32[32,1024]{1,0:T(8,128)S(1)} %bitcast.5, f32[64,1024]{1,0:T(8,128)S(1)} %bitcast.4, f32[1024,128]{1,0:T(8,128)S(1)} %copy-done, f32[3,1024,256]{2,1,0:T(8,128)} %grads_hbm.1, f32[32,256]{1,0:T(8,128)S(1)} %copy-done.5, f32[64,256]{1,0:T(8,128)S(1)} %copy-done.4, ...), custom_call_target="tpu_custom_call" | custom-call | flops 4000000000 | bytes 8000000 | tf_op jit(solution)/shard_map/step_and_route/pallas_call | solution.py:274
  56.4 4.5 %project.1 = bf16[1536,768]{1,0:T(8,128)(2,1)} custom-call(f32[128,24,128]{2,1,0:T(8,128)S(1)} %get-tuple-element.7.recv_ref, bf16[384,768]{1,0:T(8,128)(2,1)S(1)} %get-tuple-element.8.weights_ref), custom_call_target="tpu_custom_call" | custom-call | flops 1000000000 | bytes 5000000 | tf_op jit(solution)/shard_map/project/pallas_call | solution.py:318
Async XLA Ops:
  0.0 1.0 %copy-start = (f32[1024,128]{1,0:T(8,128)S(1)}, f32[1024,128]{1,0:T(8,128)}, u32[]{:S(2)}) copy-start(f32[1024,128]{1,0:T(8,128)} %wide_hbm.1) | copy-start | bytes 1572868
  1.0 0.9 %copy-start.1 = (f32[1024,64]{0,1:T(8,128)S(1)}, f32[1024,64]{0,1:T(8,128)}, u32[]{:S(2)}) copy-start(f32[1024,64]{0,1:T(8,128)} %param.10) | copy-start | bytes 786436
  2.0 0.9 %copy-start.2 = (f32[1024,32]{0,1:T(8,128)S(1)}, f32[1024,32]{0,1:T(8,128)}, u32[]{:S(2)}) copy-start(f32[1024,32]{0,1:T(8,128)} %param.9) | copy-start | bytes 393220
  2.9 0.9 %copy-start.3 = (f32[128,256]{1,0:T(8,128)S(1)}, f32[128,256]{1,0:T(8,128)}, u32[]{:S(2)}) copy-start(f32[128,256]{1,0:T(8,128)} %pw_hbm.1) | copy-start | bytes 393220
  3.8 0.8 %copy-start.4 = (f32[64,256]{1,0:T(8,128)S(1)}, f32[64,256]{1,0:T(8,128)}, u32[]{:S(2)}) copy-start(f32[64,256]{1,0:T(8,128)} %pm_hbm.1) | copy-start | bytes 196612
  4.6 0.8 %copy-start.5 = (f32[32,256]{1,0:T(8,128)S(1)}, f32[32,256]{1,0:T(8,128)}, u32[]{:S(2)}) copy-start(f32[32,256]{1,0:T(8,128)} %ps_hbm.1) | copy-start | bytes 98308
  5.4 0.7 %copy-start.6 = (s32[3,1024,1]{1,2,0:T(1,128)S(1)}, s32[3,1024,1]{1,2,0:T(1,128)}, u32[]{:S(2)}) copy-start(s32[3,1024,1]{1,2,0:T(1,128)} %param.17) | copy-start | bytes 36868
  6.1 0.7 %copy-start.7 = (s32[3,1]{0,1:T(1,128)S(1)}, s32[3,1]{0,1:T(1,128)}, u32[]{:S(2)}) copy-start(s32[3,1]{0,1:T(1,128)} %param.16) | copy-start | bytes 40

commit v2 on v1

v2 whole, which is shorter than its diff:
```python
import functools

import jax
import jax.numpy as jnp
from jax import lax
from jax.experimental import pallas as pl
from jax.experimental.pallas import tpu as pltpu
from jax.sharding import PartitionSpec as P

STEP_NORM = 16.0
ROW_RATE = 0.1
MESH = pl.DeviceIdType.MESH
N_ROWS = 16
N_SERVE = 8
DEVS = 128
CAP = 12
SLOTS = DEVS * CAP
ROWS = 1024
D = 256
LANES = 128
GROUP = 16
CHUNK = GROUP * CAP
CHUNKS = DEVS // GROUP
SHARE = 7
FINE = 64
F32 = jnp.float32
BF16 = jnp.bfloat16


def split(x):
    high = x.astype(BF16)
    low = (x - high.astype(F32)).astype(BF16)
    return high, low


def dot(a, b):
    return lax.dot_general(a, b, (((1,), (0,)), ((), ())), preferred_element_type=F32)


def dot_nt(a, b):
    return lax.dot_general(a, b, (((1,), (1,)), ((), ())), preferred_element_type=F32)


def scale_code(size):
    code = jnp.ceil(jnp.log2(jnp.maximum(size, 2.0 ** -109)) * FINE)
    return jnp.minimum(jnp.maximum(code, -110.0 * FINE), 128.0 * FINE)


def scale_up(code):
    return jnp.exp2(15.0 - code * (1.0 / FINE))


def fixed(x, factor):
    return jnp.clip(jnp.floor(x * factor + 0.5), -32767.0, 32767.0)


def front_kernel(
    small_hbm, mid_hbm, wide_hbm, grads_hbm, ps_hbm, pm_hbm, pw_hbm, counts_ref, owners_hbm,
    recv_hbm, weights_ref,
    small, mid, wide, grads, ps, pm, pw, owners,
    placed_w, placed_m, placed_s, targets, send, totals, stage1, sum1, stage2, full,
    in_sem, send_sem, recv_sem, red_send, red_recv, own_sem,
):
    rows_at = lax.axis_index("rows")
    serve_at = lax.axis_index("serve")
    me = rows_at * N_SERVE + serve_at
    z, y, x, core = rows_at // 4, rows_at % 4, serve_at // 2, serve_at % 2
    zs = [(z + d) % 4 * 4 for d in range(4)]
    ys = [(y + d) % 4 for d in range(4)]
    xs = [(x + d) % 4 * 2 for d in range(4)]
    cores = [core, 1 - core]

    sources = (owners_hbm, small_hbm, mid_hbm, wide_hbm, ps_hbm, pm_hbm, pw_hbm)
    holders = (owners, small, mid, wide, ps, pm, pw)
    loads = [pltpu.make_async_copy(s, h, in_sem.at[i]) for i, (s, h) in enumerate(zip(sources, holders))]
    grad_loads = [
        pltpu.make_async_copy(grads_hbm.at[t], grads.at[t], in_sem.at[len(loads) + t]) for t in range(3)
    ]
    for load in loads:
        load.start()
    for t in (2, 1, 0):
        grad_loads[t].start()

    barrier = pltpu.get_barrier_semaphore()
    for r in range(1, DEVS):
        pl.semaphore_signal(
            barrier, inc=1, device_id_type=MESH,
            device_id=(zs[r // 32] + ys[r // 8 % 4], xs[r // 2 % 4] + cores[r % 2]),
        )

    loads[0].wait()
    lane = lax.broadcasted_iota(jnp.int32, (1, ROWS), 1)
    named = lax.broadcasted_iota(jnp.int32, (DEVS, ROWS), 0)
    hits = []
    for t in range(3):
        live = lane < counts_ref[0, t]
        owner = jnp.where(live, owners[t], -1)
        hits.append(jnp.where(named == owner, 1.0, 0.0).astype(BF16))
    hit = jnp.concatenate(hits, axis=0)
    ahead = lax.broadcasted_iota(jnp.int32, (256, 256), 0) < lax.broadcasted_iota(jnp.int32, (256, 256), 1)
    ahead = jnp.where(ahead, 1.0, 0.0).astype(BF16)
    carry = jnp.zeros((3 * DEVS, 1), F32)
    ranks = []
    for c in range(ROWS // 256):
        part = hit[:, c * 256:(c + 1) * 256]
        before = dot(part, ahead) + carry
        mine = part.astype(F32)
        carry = before[:, 255:256] + mine[:, 255:256]
        ranks.append(jnp.sum((before * mine).reshape(3, DEVS, 256), axis=1))
    rank = jnp.concatenate(ranks, axis=1).astype(jnp.int32)
    for t in range(3):
        owner = owners[t]
        dz, dy = ((owner >> 5) - z) & 3, ((owner >> 3) - y) & 3
        dx, dc = ((owner >> 1) - x) & 3, (owner - core) & 1
        chunk = (3 - ((dy >> 1) * 2 + (dx >> 1))) * 2 + dc
        block = chunk * GROUP + dz * 4 + (dy & 1) * 2 + (dx & 1)
        live = lane < counts_ref[0, t]
        targets[t] = jnp.where(live, block * CAP + rank[t:t + 1], -1)

    for load in loads[1:]:
        load.wait()
    wide_t = wide[...].T
    both_t = jnp.concatenate([mid[...], small[...], jnp.zeros((32, ROWS), F32)], axis=0)
    both = both_t.T
    column = lax.broadcasted_iota(jnp.int32, (ROWS, LANES), 1)
    zeros = lambda n: jnp.zeros((n, D), F32)
    tiers = (
        (2, wide_t, wide[...], pw[...], placed_w),
        (1, mid[...], jnp.where(column < 64, both, 0.0),
         jnp.concatenate([pm[...], zeros(64)], axis=0), placed_m),
        (0, small[...], jnp.where(column >= 64, both, 0.0),
         jnp.concatenate([zeros(64), ps[...], zeros(32)], axis=0), placed_s),
    )
    at = 0
    row = lax.broadcasted_iota(jnp.int32, (ROWS, D), 0)
    for t, table_t, table, projection, placed in tiers:
        grad_loads[t].wait()
        masked = jnp.where(row < counts_ref[0, t], grads[t], 0.0)
        g_high, g_low = split(masked)
        e_high, e_low = split(table_t)
        total = dot(e_high, g_high) + (dot(e_low, g_high) + dot(e_high, g_low))
        slabs = table_t.shape[0] // 4
        totals[at:at + slabs] = total[:, :LANES].reshape(slabs, 4, LANES)
        totals[at + slabs:at + 2 * slabs] = total[:, LANES:].reshape(slabs, 4, LANES)
        at += 2 * slabs
        p_high, p_low = split(projection)
        step = dot_nt(g_high, p_high) + (dot_nt(g_low, p_high) + dot_nt(g_high, p_low))
        moved = table - ROW_RATE * step
        high, low = split(moved)
        placed[:, :LANES] = high
        placed[:, LANES:] = low

    pl.semaphore_wait(barrier, DEVS - 1)

    def share_of(ref, p):
        return ref.at[pl.ds(p * SHARE, SHARE)]

    for j in range(1, N_ROWS):
        p = zs[j // 4] + ys[j % 4]
        pltpu.make_async_remote_copy(
            share_of(totals, p), stage1.at[rows_at], red_send.at[0], red_recv.at[0],
            device_id=(p, serve_at), device_id_type=MESH,
        ).start()

    slot_row = lax.broadcasted_iota(jnp.int32, (CHUNK, ROWS), 0)
    column = lax.broadcasted_iota(jnp.int32, (CHUNK, LANES), 1)

    def place(c, carry):
        base = c * CHUNK

        def chosen(t):
            return jnp.where(slot_row == targets[t] - base, 1.0, 0.0).astype(BF16)

        got_a = dot(chosen(2), placed_w[...])
        got_b = dot(chosen(1), placed_m[...]) + dot(chosen(0), placed_s[...])
        a = got_a[:, :LANES] + got_a[:, LANES:]
        b = got_b[:, :LANES] + got_b[:, LANES:]
        size = jnp.abs(b)
        codes = [
            scale_code(jnp.max(part, axis=1, keepdims=True))
            for part in (jnp.abs(a), jnp.where(column < 64, size, 0.0), jnp.where(column >= 64, size, 0.0))
        ]
        a = fixed(a, scale_up(codes[0]))
        b = fixed(b, jnp.where(column < 64, scale_up(codes[1]), scale_up(codes[2])))
        for i, code in enumerate(codes):
            b = jnp.where(column == 96 + i, code, b)
        packed = (a.astype(jnp.int32) << 16) | (b.astype(jnp.int32) & 0xFFFF)
        send[pl.ds(c * GROUP, GROUP)] = packed.reshape(GROUP, 3, 4, LANES)

        left = 3 - c // 2
        y_at = [(y + left // 2 * 2 + d) % 4 for d in range(2)]
        x_at = [(x + left % 2 * 2 + d) % 4 * 2 for d in range(2)]
        core_at = (core + c) % 2
        for w in range(GROUP):
            copy = pltpu.make_async_remote_copy(
                send.at[c * GROUP + w], recv_hbm.at[me], send_sem, recv_sem,
                device_id=(zs[w // 4] + y_at[w // 2 % 2], x_at[w % 2] + core_at), device_id_type=MESH,
            )
            if w == 0:
                pl.when(c != 6)(copy.start)
            else:
                copy.start()
        return carry

    lax.fori_loop(0, CHUNKS, place, 0)
    own = pltpu.make_async_copy(send.at[6 * GROUP], recv_hbm.at[me], own_sem)
    own.start()

    def all_of(ref, n, sem):
        pltpu.make_async_copy(ref.at[pl.ds(0, n)], ref.at[pl.ds(0, n)], sem).wait()

    stage1[rows_at] = totals[pl.ds(rows_at * SHARE, SHARE)]
    all_of(stage1, N_ROWS - 1, red_recv.at[0])
    sum1[...] = jnp.sum(stage1[...], axis=0)
    for j in range(1, N_SERVE):
        pltpu.make_async_remote_copy(
            sum1, stage2.at[serve_at], red_send.at[1], red_recv.at[1],
            device_id=(rows_at, xs[j // 2] + cores[j % 2]), device_id_type=MESH,
        ).start()
    stage2[serve_at] = sum1[...]
    all_of(stage2, N_SERVE - 1, red_recv.at[1])
    full[rows_at] = jnp.sum(stage2[...], axis=0)
    for j in range(1, N_ROWS):
        pltpu.make_async_remote_copy(
            full.at[rows_at], full.at[rows_at], red_send.at[2], red_recv.at[2],
            device_id=(zs[j // 4] + ys[j % 4], serve_at), device_id_type=MESH,
        ).start()
    all_of(full, N_ROWS - 1, red_recv.at[2])

    summed = full[...].reshape(N_ROWS * SHARE * 4, LANES)
    at = 0
    fresh = []
    for projection in (pw[...], pm[...], ps[...]):
        width = projection.shape[0]
        total = jnp.concatenate([summed[at:at + width], summed[at + width:at + 2 * width]], axis=1)
        at += 2 * width
        size = jnp.sum(total * total, axis=(0, 1), keepdims=True)
        fresh.append(projection - (STEP_NORM / jnp.sqrt(size + 1e-06)) * total)
    columns = (
        jnp.concatenate([zeros(64), fresh[2], zeros(32)], axis=0),
        jnp.concatenate([fresh[1], zeros(64)], axis=0),
        fresh[0],
    )
    for t in range(3):
        high, low = split(columns[t])
        weights_ref[0:128, t * D:(t + 1) * D] = high
        weights_ref[128:256, t * D:(t + 1) * D] = high
        weights_ref[256:384, t * D:(t + 1) * D] = low

    own.wait()
    all_of(recv_hbm, DEVS - 1, recv_sem)
    all_of(send, DEVS - 1, send_sem)
    all_of(stage1, N_ROWS - 1, red_send.at[0])
    all_of(stage2, N_SERVE - 1, red_send.at[1])
    all_of(full, N_ROWS - 1, red_send.at[2])


def project_kernel(recv_ref, weights_ref, out_ref):
    packed = recv_ref[...]
    b = (packed << 16) >> 16
    code = b[:, 96:99].astype(F32)
    down = 1.0 / scale_up(code)
    column = lax.broadcasted_iota(jnp.int32, packed.shape, 1)
    a = (packed >> 16).astype(F32) * down[:, 0:1]
    b = b.astype(F32) * jnp.where(column < 64, down[:, 1:2], jnp.where(column < 96, down[:, 2:3], 0.0))
    for rows, first, last in ((b, 0, 2 * D), (a, 2 * D, 3 * D)):
        high, low = split(rows)
        both = jnp.concatenate([high, low, high], axis=1)
        out_ref[:, first:last] = dot(both, weights_ref[:, first:last]).astype(BF16)


def local(rows_small, rows_mid, rows_wide, row_grads, proj_small, proj_mid, proj_wide, counts, owners):
    hbm = pl.BlockSpec(memory_space=pl.ANY)
    vmem = pl.BlockSpec(memory_space=pltpu.VMEM)
    recv, weights = pl.pallas_call(
        front_kernel,
        out_shape=(
            jax.ShapeDtypeStruct((DEVS, 3, 4, LANES), jnp.int32),
            jax.ShapeDtypeStruct((384, 3 * D), BF16),
        ),
        in_specs=[hbm] * 7 + [pl.BlockSpec(memory_space=pltpu.SMEM), hbm],
        out_specs=(hbm, vmem),
        scratch_shapes=[
            pltpu.VMEM((32, ROWS), F32),
            pltpu.VMEM((64, ROWS), F32),
            pltpu.VMEM((ROWS, LANES), F32),
            pltpu.VMEM((3, ROWS, D), F32),
            pltpu.VMEM((32, D), F32),
            pltpu.VMEM((64, D), F32),
            pltpu.VMEM((128, D), F32),
            pltpu.VMEM((3, 1, ROWS), jnp.int32),
            pltpu.VMEM((ROWS, 2 * LANES), BF16),
            pltpu.VMEM((ROWS, 2 * LANES), BF16),
            pltpu.VMEM((ROWS, 2 * LANES), BF16),
            pltpu.VMEM((3, 1, ROWS), jnp.int32),
            pltpu.VMEM((DEVS, 3, 4, LANES), jnp.int32),
            pltpu.VMEM((N_ROWS * SHARE, 4, LANES), F32),
            pltpu.VMEM((N_ROWS, SHARE, 4, LANES), F32),
            pltpu.VMEM((SHARE, 4, LANES), F32),
            pltpu.VMEM((N_SERVE, SHARE, 4, LANES), F32),
            pltpu.VMEM((N_ROWS, SHARE, 4, LANES), F32),
            pltpu.SemaphoreType.DMA((10,)),
            pltpu.SemaphoreType.DMA,
            pltpu.SemaphoreType.DMA,
            pltpu.SemaphoreType.DMA((3,)),
            pltpu.SemaphoreType.DMA((3,)),
            pltpu.SemaphoreType.DMA,
        ],
        compiler_params=pltpu.CompilerParams(
            collective_id=0, has_side_effects=True, vmem_limit_bytes=64 << 20
        ),
        cost_estimate=pl.CostEstimate(flops=4_000_000_000, bytes_accessed=8_000_000, transcendentals=0),
        name="step_and_route",
    )(
        rows_small.T, rows_mid.T, rows_wide, row_grads, proj_small, proj_mid, proj_wide,
        counts.T, jnp.transpose(owners, (0, 2, 1)),
    )
    part = 192
    return pl.pallas_call(
        project_kernel,
        grid=(SLOTS // part,),
        out_shape=jax.ShapeDtypeStruct((SLOTS, 3 * D), BF16),
        in_specs=[
            pl.BlockSpec((part, LANES), lambda i: (i, 0)),
            pl.BlockSpec((384, 3 * D), lambda i: (0, 0)),
        ],
        out_specs=pl.BlockSpec((part, 3 * D), lambda i: (i, 0)),
        compiler_params=pltpu.CompilerParams(vmem_limit_bytes=64 << 20),
        cost_estimate=pl.CostEstimate(flops=1_000_000_000, bytes_accessed=5_000_000, transcendentals=0),
        name="project",
    )(recv.reshape(SLOTS, LANES), weights)


def solution(mesh):
    return jax.shard_map(
        local,
        mesh=mesh,
        in_specs=(
            P(("rows", "serve"), None),
            P(("rows", "serve"), None),
            P(("rows", "serve"), None),
            P(None, ("rows", "serve"), None),
            P(),
            P(),
            P(),
            P(None, ("rows", "serve")),
            P(None, ("rows", "serve"), None),
        ),
        out_specs=P(("rows", "serve"), None),
        check_vma=False,
    )
```

time: 61.2 us -> 43.2 us (0.71)
  Pallas kernels: 54.1 us -> 42.7 us
  local copies, waits for them, and re-layouts: 6.76 us -> 0 us
    pallas_call x2, Pallas kernels: 54.1 us -> 42.7 us  [the longest x1 35.6 us: local(): pl.pallas_call(front_kernel, out_shape=(jax.ShapeDtypeStruct((DEVS, 3, 4,...]
    unnamed x16 -> x0, local copies, waits for them, and re-layouts: 6.76 us -> none
where the time goes in v2:
time: 43.2 us; the launch traced here: 42.7 us
  Pallas kernels  42.7 us (99%)
    pallas_call x1, Pallas kernels, local(): pl.pallas_call(front_kernel, out_shape=(jax.ShapeDtypeStruct((DEVS, 3, 4,...  35.6 us
    pallas_call x1, Pallas kernels, local(): pl.pallas_call(project_kernel, grid=(SLOTS // part,), out_shape=jax.Shape...  7.07 us

profile of v2, /device:TPU:1, one launch (start us, length us, event | category | flops | bytes accessed | tf_op | source)
XLA Modules:
  0.0 42.7 jit_solution(11297568883185010480)
XLA Ops:
  0.0 35.6 %step_and_route.1 = (s32[128,3,4,128]{3,2,1,0:T(4,128)}, bf16[384,768]{1,0:T(8,128)(2,1)}) custom-call(f32[32,1024]{1,0:T(8,128)} %bitcast.7, f32[64,1024]{1,0:T(8,128)} %bitcast.6, f32[1024,128]{1,0:T(8,128)} %wide_hbm.1, f32[3,1024,256]{2,1,0:T(8,128)} %grads_hbm.1, f32[32,256]{1,0:T(8,128)} %ps_hbm.1, f32[64,256]{1,0:T(8,128)} %pm_hbm.1, ...), custom_call_target="tpu_custom_call" | custom-call | flops 4000000000 | bytes 8000000 | tf_op jit(solution)/shard_map/step_and_route/pallas_call | solution.py:275
  35.6 7.1 %project.1 = bf16[1536,768]{1,0:T(8,128)(2,1)} custom-call(s32[1536,128]{1,0:T(8,128)} %bitcast.5, bf16[384,768]{1,0:T(8,128)(2,1)} %get-tuple-element.8.weights_ref), custom_call_target="tpu_custom_call" | custom-call | flops 1000000000 | bytes 5000000 | tf_op jit(solution)/shard_map/project/pallas_call | solution.py:319

commit v3 on v2

--- a/solution.py
+++ b/solution.py
@@ -10,6 +10,7 @@
 STEP_NORM = 16.0
 ROW_RATE = 0.1
 MESH = pl.DeviceIdType.MESH
+FAR_FIRST = sorted(range(1, 16), key=lambda j: -(min(j // 4, 4 - j // 4) + min(j % 4, 4 - j % 4)))
 N_ROWS = 16
 N_SERVE = 8
 DEVS = 128
@@ -23,6 +24,12 @@
 CHUNKS = DEVS // GROUP
 SHARE = 7
 FINE = 64
+SELF_GROUP = 6
+EARLY = 6
+MIDDLE = 8
+PARTS = 4
+STRIPE = 768
+PART = SLOTS // PARTS
 F32 = jnp.float32
 BF16 = jnp.bfloat16
 
@@ -56,10 +63,10 @@
 
 def front_kernel(
     small_hbm, mid_hbm, wide_hbm, grads_hbm, ps_hbm, pm_hbm, pw_hbm, counts_ref, owners_hbm,
-    recv_hbm, weights_ref,
+    spread_hbm, weights_ref,
     small, mid, wide, grads, ps, pm, pw, owners,
-    placed_w, placed_m, placed_s, targets, send, totals, stage1, sum1, stage2, full,
-    in_sem, send_sem, recv_sem, red_send, red_recv, own_sem,
+    parts, placed_w, placed_m, placed_s, targets, send, recv, spread, totals, stage1, sum1, stage2, full,
+    in_sem, send_sem, recv_sem, red_send, red_recv, own_sem, out_sem,
 ):
     rows_at = lax.axis_index("rows")
     serve_at = lax.axis_index("serve")
@@ -76,10 +83,8 @@
     grad_loads = [
         pltpu.make_async_copy(grads_hbm.at[t], grads.at[t], in_sem.at[len(loads) + t]) for t in range(3)
     ]
-    for load in loads:
+    for load in loads[3:4] + grad_loads[2:] + loads[1:3] + grad_loads[1::-1] + loads[4:] + loads[:1]:
         load.start()
-    for t in (2, 1, 0):
-        grad_loads[t].start()
 
     barrier = pltpu.get_barrier_semaphore()
     for r in range(1, DEVS):
@@ -87,6 +92,47 @@
             barrier, inc=1, device_id_type=MESH,
             device_id=(zs[r // 32] + ys[r // 8 % 4], xs[r // 2 % 4] + cores[r % 2]),
         )
+
+    for load in loads[1:]:
+        load.wait()
+    wide_t = wide[...].T
+    both_t = jnp.concatenate([mid[...], small[...], jnp.zeros((32, ROWS), F32)], axis=0)
+    both = both_t.T
+    column = lax.broadcasted_iota(jnp.int32, (ROWS, LANES), 1)
+    zeros = lambda n: jnp.zeros((n, D), F32)
+    tiers = (
+        (2, wide_t, wide[...], pw[...], placed_w),
+        (1, mid[...], jnp.where(column < 64, both, 0.0),
+         jnp.concatenate([pm[...], zeros(64)], axis=0), placed_m),
+        (0, small[...], jnp.where(column >= 64, both, 0.0),
+         jnp.concatenate([zeros(64), ps[...], zeros(32)], axis=0), placed_s),
+    )
+    at = 0
+    row = lax.broadcasted_iota(jnp.int32, (ROWS, D), 0)
+    for t, table_t, table, projection, placed in tiers:
+        grad_loads[t].wait()
+        masked = jnp.where(row < counts_ref[0, t], grads[t], 0.0)
+        g_high, g_low = split(masked)
+        parts[t, :, :D] = g_high
+        parts[t, :, D:] = g_low
+        e_high, e_low = split(table_t)
+        total = dot(e_high, g_high) + (dot(e_low, g_high) + dot(e_high, g_low))
+        slabs = table_t.shape[0] // 4
+        totals[at:at + slabs] = total[:, :LANES].reshape(slabs, 4, LANES)
+        totals[at + slabs:at + 2 * slabs] = total[:, LANES:].reshape(slabs, 4, LANES)
+        at += 2 * slabs
+
+    pl.semaphore_wait(barrier, DEVS - 1)
+
+    def share_of(ref, p):
+        return ref.at[pl.ds(p * SHARE, SHARE)]
+
+    for j in FAR_FIRST:
+        p = zs[j // 4] + ys[j % 4]
+        pltpu.make_async_remote_copy(
+            share_of(totals, p), stage1.at[rows_at], red_send.at[0], red_recv.at[0],
+            device_id=(p, serve_at), device_id_type=MESH,
+        ).start()
 
     loads[0].wait()
     lane = lax.broadcasted_iota(jnp.int32, (1, ROWS), 1)
@@ -117,32 +163,8 @@
         live = lane < counts_ref[0, t]
         targets[t] = jnp.where(live, block * CAP + rank[t:t + 1], -1)
 
-    for load in loads[1:]:
-        load.wait()
-    wide_t = wide[...].T
-    both_t = jnp.concatenate([mid[...], small[...], jnp.zeros((32, ROWS), F32)], axis=0)
-    both = both_t.T
-    column = lax.broadcasted_iota(jnp.int32, (ROWS, LANES), 1)
-    zeros = lambda n: jnp.zeros((n, D), F32)
-    tiers = (
-        (2, wide_t, wide[...], pw[...], placed_w),
-        (1, mid[...], jnp.where(column < 64, both, 0.0),
-         jnp.concatenate([pm[...], zeros(64)], axis=0), placed_m),
-        (0, small[...], jnp.where(column >= 64, both, 0.0),
-         jnp.concatenate([zeros(64), ps[...], zeros(32)], axis=0), placed_s),
-    )
-    at = 0
-    row = lax.broadcasted_iota(jnp.int32, (ROWS, D), 0)
     for t, table_t, table, projection, placed in tiers:
-        grad_loads[t].wait()
-        masked = jnp.where(row < counts_ref[0, t], grads[t], 0.0)
-        g_high, g_low = split(masked)
-        e_high, e_low = split(table_t)
-        total = dot(e_high, g_high) + (dot(e_low, g_high) + dot(e_high, g_low))
-        slabs = table_t.shape[0] // 4
-        totals[at:at + slabs] = total[:, :LANES].reshape(slabs, 4, LANES)
-        totals[at + slabs:at + 2 * slabs] = total[:, LANES:].reshape(slabs, 4, LANES)
-        at += 2 * slabs
+        g_high, g_low = parts[t, :, :D], parts[t, :, D:]
         p_high, p_low = split(projection)
         step = dot_nt(g_high, p_high) + (dot_nt(g_low, p_high) + dot_nt(g_high, p_low))
         moved = table - ROW_RATE * step
@@ -150,22 +172,10 @@
         placed[:, :LANES] = high
         placed[:, LANES:] = low
 
-    pl.semaphore_wait(barrier, DEVS - 1)
-
-    def share_of(ref, p):
-        return ref.at[pl.ds(p * SHARE, SHARE)]
-
-    for j in range(1, N_ROWS):
-        p = zs[j // 4] + ys[j % 4]
-        pltpu.make_async_remote_copy(
-            share_of(totals, p), stage1.at[rows_at], red_send.at[0], red_recv.at[0],
-            device_id=(p, serve_at), device_id_type=MESH,
-        ).start()
-
     slot_row = lax.broadcasted_iota(jnp.int32, (CHUNK, ROWS), 0)
     column = lax.broadcasted_iota(jnp.int32, (CHUNK, LANES), 1)
 
-    def place(c, carry):
+    def place(c):
         base = c * CHUNK
 
         def chosen(t):
@@ -187,23 +197,31 @@
         packed = (a.astype(jnp.int32) << 16) | (b.astype(jnp.int32) & 0xFFFF)
         send[pl.ds(c * GROUP, GROUP)] = packed.reshape(GROUP, 3, 4, LANES)
 
+    def send_group(c):
         left = 3 - c // 2
         y_at = [(y + left // 2 * 2 + d) % 4 for d in range(2)]
         x_at = [(x + left % 2 * 2 + d) % 4 * 2 for d in range(2)]
         core_at = (core + c) % 2
         for w in range(GROUP):
-            copy = pltpu.make_async_remote_copy(
-                send.at[c * GROUP + w], recv_hbm.at[me], send_sem, recv_sem,
+            if c is SELF_GROUP and w == 0:
+                continue
+            pltpu.make_async_remote_copy(
+                send.at[c * GROUP + w], recv.at[me], send_sem, recv_sem,
                 device_id=(zs[w // 4] + y_at[w // 2 % 2], x_at[w % 2] + core_at), device_id_type=MESH,
-            )
-            if w == 0:
-                pl.when(c != 6)(copy.start)
-            else:
-                copy.start()
+            ).start()
+
+    def place_and_send(c, carry):
+        place(c)
+        send_group(c)
         return carry
 
-    lax.fori_loop(0, CHUNKS, place, 0)
-    own = pltpu.make_async_copy(send.at[6 * GROUP], recv_hbm.at[me], own_sem)
+    def place_only(c, carry):
+        place(c)
+        return carry
+
+    lax.fori_loop(0, EARLY, place_and_send, 0)
+    lax.fori_loop(EARLY, CHUNKS, place_only, 0)
+    own = pltpu.make_async_copy(send.at[SELF_GROUP * GROUP], recv.at[me], own_sem)
     own.start()
 
     def all_of(ref, n, sem):
@@ -212,19 +230,40 @@
     stage1[rows_at] = totals[pl.ds(rows_at * SHARE, SHARE)]
     all_of(stage1, N_ROWS - 1, red_recv.at[0])
     sum1[...] = jnp.sum(stage1[...], axis=0)
-    for j in range(1, N_SERVE):
+    for j in (4, 5, 2, 3, 6, 7, 1):
         pltpu.make_async_remote_copy(
             sum1, stage2.at[serve_at], red_send.at[1], red_recv.at[1],
             device_id=(rows_at, xs[j // 2] + cores[j % 2]), device_id_type=MESH,
         ).start()
+    for c in range(EARLY, MIDDLE):
+        send_group(c)
     stage2[serve_at] = sum1[...]
     all_of(stage2, N_SERVE - 1, red_recv.at[1])
     full[rows_at] = jnp.sum(stage2[...], axis=0)
-    for j in range(1, N_ROWS):
+    for j in FAR_FIRST:
         pltpu.make_async_remote_copy(
             full.at[rows_at], full.at[rows_at], red_send.at[2], red_recv.at[2],
             device_id=(zs[j // 4] + ys[j % 4], serve_at), device_id_type=MESH,
         ).start()
+    for c in range(MIDDLE, CHUNKS):
+        send_group(c)
+    own.wait()
+    all_of(recv, DEVS - 1, recv_sem)
+    column = lax.broadcasted_iota(jnp.int32, (PART, LANES), 1)
+    for i in range(PARTS):
+        part = pl.ds(i * PART, PART)
+        packed = recv[i * PART // CAP:(i + 1) * PART // CAP].reshape(PART, LANES)
+        b = (packed << 16) >> 16
+        down = 1.0 / scale_up(b[:, 96:99].astype(F32))
+        a = (packed >> 16).astype(F32) * down[:, 0:1]
+        b = b.astype(F32) * jnp.where(column < 64, down[:, 1:2], jnp.where(column < 96, down[:, 2:3], 0.0))
+        for k, rows in enumerate((a, b)):
+            high, low = split(rows)
+            spread[k, part, :LANES] = high
+            spread[k, part, LANES:] = low
+    kept = pltpu.make_async_copy(spread, spread_hbm, out_sem)
+    kept.start()
+
     all_of(full, N_ROWS - 1, red_recv.at[2])
 
     summed = full[...].reshape(N_ROWS * SHARE * 4, LANES)
@@ -244,39 +283,30 @@
     for t in range(3):
         high, low = split(columns[t])
         weights_ref[0:128, t * D:(t + 1) * D] = high
-        weights_ref[128:256, t * D:(t + 1) * D] = high
-        weights_ref[256:384, t * D:(t + 1) * D] = low
-
-    own.wait()
-    all_of(recv_hbm, DEVS - 1, recv_sem)
+        weights_ref[128:256, t * D:(t + 1) * D] = low
+
+    kept.wait()
     all_of(send, DEVS - 1, send_sem)
     all_of(stage1, N_ROWS - 1, red_send.at[0])
     all_of(stage2, N_SERVE - 1, red_send.at[1])
     all_of(full, N_ROWS - 1, red_send.at[2])
 
 
-def project_kernel(recv_ref, weights_ref, out_ref):
-    packed = recv_ref[...]
-    b = (packed << 16) >> 16
-    code = b[:, 96:99].astype(F32)
-    down = 1.0 / scale_up(code)
-    column = lax.broadcasted_iota(jnp.int32, packed.shape, 1)
-    a = (packed >> 16).astype(F32) * down[:, 0:1]
-    b = b.astype(F32) * jnp.where(column < 64, down[:, 1:2], jnp.where(column < 96, down[:, 2:3], 0.0))
-    for rows, first, last in ((b, 0, 2 * D), (a, 2 * D, 3 * D)):
-        high, low = split(rows)
-        both = jnp.concatenate([high, low, high], axis=1)
-        out_ref[:, first:last] = dot(both, weights_ref[:, first:last]).astype(BF16)
+def project_kernel(spread_ref, weights_ref, out_ref):
+    for k, first, last in ((1, 0, 2 * D), (0, 2 * D, 3 * D)):
+        high, low = weights_ref[:LANES, first:last], weights_ref[LANES:, first:last]
+        both = jnp.concatenate([high, high], axis=0)
+        out_ref[:, first:last] = (dot(spread_ref[k], both) + dot(spread_ref[k, :, :LANES], low)).astype(BF16)
 
 
 def local(rows_small, rows_mid, rows_wide, row_grads, proj_small, proj_mid, proj_wide, counts, owners):
     hbm = pl.BlockSpec(memory_space=pl.ANY)
     vmem = pl.BlockSpec(memory_space=pltpu.VMEM)
-    recv, weights = pl.pallas_call(
+    spread, weights = pl.pallas_call(
         front_kernel,
         out_shape=(
-            jax.ShapeDtypeStruct((DEVS, 3, 4, LANES), jnp.int32),
-            jax.ShapeDtypeStruct((384, 3 * D), BF16),
+            jax.ShapeDtypeStruct((2, SLOTS, 2 * LANES), BF16),
+            jax.ShapeDtypeStruct((2 * LANES, 3 * D), BF16),
         ),
         in_specs=[hbm] * 7 + [pl.BlockSpec(memory_space=pltpu.SMEM), hbm],
         out_specs=(hbm, vmem),
@@ -289,11 +319,14 @@
             pltpu.VMEM((64, D), F32),
             pltpu.VMEM((128, D), F32),
             pltpu.VMEM((3, 1, ROWS), jnp.int32),
+            pltpu.VMEM((3, ROWS, 2 * D), BF16),
             pltpu.VMEM((ROWS, 2 * LANES), BF16),
             pltpu.VMEM((ROWS, 2 * LANES), BF16),
             pltpu.VMEM((ROWS, 2 * LANES), BF16),
             pltpu.VMEM((3, 1, ROWS), jnp.int32),
             pltpu.VMEM((DEVS, 3, 4, LANES), jnp.int32),
+            pltpu.VMEM((DEVS, 3, 4, LANES), jnp.int32),
+            pltpu.VMEM((2, SLOTS, 2 * LANES), BF16),
             pltpu.VMEM((N_ROWS * SHARE, 4, LANES), F32),
             pltpu.VMEM((N_ROWS, SHARE, 4, LANES), F32),
             pltpu.VMEM((SHARE, 4, LANES), F32),
@@ -305,6 +338,7 @@
             pltpu.SemaphoreType.DMA((3,)),
             pltpu.SemaphoreType.DMA((3,)),
             pltpu.SemaphoreType.DMA,
+            pltpu.SemaphoreType.DMA,
         ],
         compiler_params=pltpu.CompilerParams(
             collective_id=0, has_side_effects=True, vmem_limit_bytes=64 << 20
@@ -315,20 +349,19 @@
         rows_small.T, rows_mid.T, rows_wide, row_grads, proj_small, proj_mid, proj_wide,
         counts.T, jnp.transpose(owners, (0, 2, 1)),
     )
-    part = 192
     return pl.pallas_call(
         project_kernel,
-        grid=(SLOTS // part,),
+        grid=(SLOTS // STRIPE,),
         out_shape=jax.ShapeDtypeStruct((SLOTS, 3 * D), BF16),
         in_specs=[
-            pl.BlockSpec((part, LANES), lambda i: (i, 0)),
-            pl.BlockSpec((384, 3 * D), lambda i: (0, 0)),
+            pl.BlockSpec((2, STRIPE, 2 * LANES), lambda i: (0, i, 0)),
+            pl.BlockSpec((2 * LANES, 3 * D), lambda i: (0, 0)),
         ],
-        out_specs=pl.BlockSpec((part, 3 * D), lambda i: (i, 0)),
+        out_specs=pl.BlockSpec((STRIPE, 3 * D), lambda i: (i, 0)),
         compiler_params=pltpu.CompilerParams(vmem_limit_bytes=64 << 20),
         cost_estimate=pl.CostEstimate(flops=1_000_000_000, bytes_accessed=5_000_000, transcendentals=0),
         name="project",
-    )(recv.reshape(SLOTS, LANES), weights)
+    )(spread, weights)
 
 
 def solution(mesh):

time: 43.2 us -> 35.9 us (0.83)
  Pallas kernels: 42.7 us -> 35.7 us
    pallas_call x2, Pallas kernels: 42.7 us -> 35.7 us  [the longest x1 31.9 us: local(): pl.pallas_call(front_kernel, out_shape=(jax.ShapeDtypeStruct((2, SLOTS, 2...]
where the time goes in v3:
time: 35.9 us; the launch traced here: 35.7 us
  Pallas kernels  35.7 us (99%)
    pallas_call x1, Pallas kernels, local(): pl.pallas_call(front_kernel, out_shape=(jax.ShapeDtypeStruct((2, SLOTS, 2...  31.9 us
    pallas_call x1, Pallas kernels, local(): pl.pallas_call(project_kernel, grid=(SLOTS // STRIPE,), out_shape=jax.Sha...  3.81 us

profile of v3, /device:TPU:1, one launch (start us, length us, event | category | flops | bytes accessed | tf_op | source)
XLA Modules:
  0.0 35.7 jit_solution(13367156600201978519)
XLA Ops:
  0.0 31.9 %step_and_route.1 = (bf16[2,1536,256]{2,1,0:T(8,128)(2,1)}, bf16[256,768]{1,0:T(8,128)(2,1)}) custom-call(f32[32,1024]{1,0:T(8,128)} %bitcast.5, f32[64,1024]{1,0:T(8,128)} %bitcast.4, f32[1024,128]{1,0:T(8,128)} %wide_hbm.1, f32[3,1024,256]{2,1,0:T(8,128)} %grads_hbm.1, f32[32,256]{1,0:T(8,128)} %ps_hbm.1, f32[64,256]{1,0:T(8,128)} %pm_hbm.1, ...), custom_call_target="tpu_custom_call" | custom-call | flops 4000000000 | bytes 8000000 | tf_op jit(solution)/shard_map/step_and_route/pallas_call | solution.py:305
  31.9 3.8 %project.1 = bf16[1536,768]{1,0:T(8,128)(2,1)} custom-call(bf16[2,1536,256]{2,1,0:T(8,128)(2,1)} %get-tuple-element.7.spread_ref, bf16[256,768]{1,0:T(8,128)(2,1)} %get-tuple-element.8.weights_ref), custom_call_target="tpu_custom_call" | custom-call | flops 1000000000 | bytes 5000000 | tf_op jit(solution)/shard_map/project/pallas_call | solution.py:352

commit v4 on v3

--- a/solution.py
+++ b/solution.py
@@ -19,17 +19,14 @@
 ROWS = 1024
 D = 256
 LANES = 128
-GROUP = 16
+GROUP = 32
 CHUNK = GROUP * CAP
 CHUNKS = DEVS // GROUP
 SHARE = 7
 FINE = 64
-SELF_GROUP = 6
-EARLY = 6
-MIDDLE = 8
-PARTS = 4
+EARLY = 2
 STRIPE = 768
-PART = SLOTS // PARTS
+PLANE = 8 * CAP
 F32 = jnp.float32
 BF16 = jnp.bfloat16
 
@@ -66,7 +63,7 @@
     spread_hbm, weights_ref,
     small, mid, wide, grads, ps, pm, pw, owners,
     parts, placed_w, placed_m, placed_s, targets, send, recv, spread, totals, stage1, sum1, stage2, full,
-    in_sem, send_sem, recv_sem, red_send, red_recv, own_sem, out_sem,
+    in_sem, send_sem, recv_sem, red_send, red_recv, out_sem,
 ):
     rows_at = lax.axis_index("rows")
     serve_at = lax.axis_index("serve")
@@ -83,7 +80,7 @@
     grad_loads = [
         pltpu.make_async_copy(grads_hbm.at[t], grads.at[t], in_sem.at[len(loads) + t]) for t in range(3)
     ]
-    for load in loads[3:4] + grad_loads[2:] + loads[1:3] + grad_loads[1::-1] + loads[4:] + loads[:1]:
+    for load in (loads[3], grad_loads[2], loads[2], grad_loads[1], loads[1], grad_loads[0], *loads[4:], loads[0]):
         load.start()
 
     barrier = pltpu.get_barrier_semaphore()
@@ -93,46 +90,24 @@
             device_id=(zs[r // 32] + ys[r // 8 % 4], xs[r // 2 % 4] + cores[r % 2]),
         )
 
-    for load in loads[1:]:
-        load.wait()
-    wide_t = wide[...].T
-    both_t = jnp.concatenate([mid[...], small[...], jnp.zeros((32, ROWS), F32)], axis=0)
-    both = both_t.T
-    column = lax.broadcasted_iota(jnp.int32, (ROWS, LANES), 1)
-    zeros = lambda n: jnp.zeros((n, D), F32)
-    tiers = (
-        (2, wide_t, wide[...], pw[...], placed_w),
-        (1, mid[...], jnp.where(column < 64, both, 0.0),
-         jnp.concatenate([pm[...], zeros(64)], axis=0), placed_m),
-        (0, small[...], jnp.where(column >= 64, both, 0.0),
-         jnp.concatenate([zeros(64), ps[...], zeros(32)], axis=0), placed_s),
-    )
     at = 0
     row = lax.broadcasted_iota(jnp.int32, (ROWS, D), 0)
-    for t, table_t, table, projection, placed in tiers:
+    for t, load, table in ((2, loads[3], wide), (1, loads[2], mid), (0, loads[1], small)):
+        load.wait()
+        table_t = wide[...].T if t == 2 else table[...]
+        width = table_t.shape[0]
+        e_high, e_low = split(table_t)
         grad_loads[t].wait()
         masked = jnp.where(row < counts_ref[0, t], grads[t], 0.0)
         g_high, g_low = split(masked)
         parts[t, :, :D] = g_high
         parts[t, :, D:] = g_low
-        e_high, e_low = split(table_t)
-        total = dot(e_high, g_high) + (dot(e_low, g_high) + dot(e_high, g_low))
-        slabs = table_t.shape[0] // 4
+        first = dot(jnp.concatenate([e_high, e_low], axis=0), g_high)
+        total = first[:width] + (first[width:] + dot(e_high, g_low))
+        slabs = width // 4
         totals[at:at + slabs] = total[:, :LANES].reshape(slabs, 4, LANES)
         totals[at + slabs:at + 2 * slabs] = total[:, LANES:].reshape(slabs, 4, LANES)
         at += 2 * slabs
-
-    pl.semaphore_wait(barrier, DEVS - 1)
-
-    def share_of(ref, p):
-        return ref.at[pl.ds(p * SHARE, SHARE)]
-
-    for j in FAR_FIRST:
-        p = zs[j // 4] + ys[j % 4]
-        pltpu.make_async_remote_copy(
-            share_of(totals, p), stage1.at[rows_at], red_send.at[0], red_recv.at[0],
-            device_id=(p, serve_at), device_id_type=MESH,
-        ).start()
 
     loads[0].wait()
     lane = lax.broadcasted_iota(jnp.int32, (1, ROWS), 1)
@@ -158,22 +133,45 @@
         owner = owners[t]
         dz, dy = ((owner >> 5) - z) & 3, ((owner >> 3) - y) & 3
         dx, dc = ((owner >> 1) - x) & 3, (owner - core) & 1
-        chunk = (3 - ((dy >> 1) * 2 + (dx >> 1))) * 2 + dc
-        block = chunk * GROUP + dz * 4 + (dy & 1) * 2 + (dx & 1)
+        chunk = (dy - dz - 1) & 3
+        block = chunk * GROUP + dz * 8 + dx * 2 + dc
         live = lane < counts_ref[0, t]
         targets[t] = jnp.where(live, block * CAP + rank[t:t + 1], -1)
 
-    for t, table_t, table, projection, placed in tiers:
+    pl.semaphore_wait(barrier, DEVS - 1)
+
+    def share_of(ref, p):
+        return ref.at[pl.ds(p * SHARE, SHARE)]
+
+    for j in FAR_FIRST:
+        p = zs[j // 4] + ys[j % 4]
+        pltpu.make_async_remote_copy(
+            share_of(totals, p), stage1.at[rows_at], red_send.at[0], red_recv.at[0],
+            device_id=(p, serve_at), device_id_type=MESH,
+        ).start()
+
+    for load in loads[4:]:
+        load.wait()
+    both = jnp.concatenate([mid[...], small[...], jnp.zeros((32, ROWS), F32)], axis=0).T
+    column = lax.broadcasted_iota(jnp.int32, (ROWS, LANES), 1)
+    zeros = lambda n: jnp.zeros((n, D), F32)
+    tiers = (
+        (2, wide[...], pw[...], placed_w),
+        (1, jnp.where(column < 64, both, 0.0), jnp.concatenate([pm[...], zeros(64)], axis=0), placed_m),
+        (0, jnp.where(column >= 64, both, 0.0), jnp.concatenate([zeros(64), ps[...], zeros(32)], axis=0), placed_s),
+    )
+    for t, table, projection, placed in tiers:
         g_high, g_low = parts[t, :, :D], parts[t, :, D:]
         p_high, p_low = split(projection)
-        step = dot_nt(g_high, p_high) + (dot_nt(g_low, p_high) + dot_nt(g_high, p_low))
-        moved = table - ROW_RATE * step
-        high, low = split(moved)
+        step = dot_nt(g_high, jnp.concatenate([p_high, p_low], axis=0))
+        step = step[:, :LANES] + (step[:, LANES:] + dot_nt(g_low, p_high))
+        high, low = split(table - ROW_RATE * step)
         placed[:, :LANES] = high
         placed[:, LANES:] = low
 
     slot_row = lax.broadcasted_iota(jnp.int32, (CHUNK, ROWS), 0)
     column = lax.broadcasted_iota(jnp.int32, (CHUNK, LANES), 1)
+    of_mid = (column < 64) | (column == 97)
 
     def place(c):
         base = c * CHUNK
@@ -186,29 +184,27 @@
         a = got_a[:, :LANES] + got_a[:, LANES:]
         b = got_b[:, :LANES] + got_b[:, LANES:]
         size = jnp.abs(b)
-        codes = [
-            scale_code(jnp.max(part, axis=1, keepdims=True))
-            for part in (jnp.abs(a), jnp.where(column < 64, size, 0.0), jnp.where(column >= 64, size, 0.0))
-        ]
-        a = fixed(a, scale_up(codes[0]))
-        b = fixed(b, jnp.where(column < 64, scale_up(codes[1]), scale_up(codes[2])))
-        for i, code in enumerate(codes):
-            b = jnp.where(column == 96 + i, code, b)
+        largest = lambda part: jnp.max(part, axis=1, keepdims=True)
+        size_a = largest(jnp.abs(a))
+        size_m, size_s = largest(jnp.where(column < 64, size, 0.0)), largest(jnp.where(column >= 64, size, 0.0))
+        code_a = scale_code(size_a)
+        code_b = scale_code(jnp.where(of_mid, size_m, size_s))
+        a = fixed(a, scale_up(code_a))
+        b = fixed(b, scale_up(code_b))
+        b = jnp.where(column < 96, b, jnp.where(column == 96, code_a, code_b))
         packed = (a.astype(jnp.int32) << 16) | (b.astype(jnp.int32) & 0xFFFF)
         send[pl.ds(c * GROUP, GROUP)] = packed.reshape(GROUP, 3, 4, LANES)
 
     def send_group(c):
-        left = 3 - c // 2
-        y_at = [(y + left // 2 * 2 + d) % 4 for d in range(2)]
-        x_at = [(x + left % 2 * 2 + d) % 4 * 2 for d in range(2)]
-        core_at = (core + c) % 2
-        for w in range(GROUP):
-            if c is SELF_GROUP and w == 0:
-                continue
-            pltpu.make_async_remote_copy(
-                send.at[c * GROUP + w], recv.at[me], send_sem, recv_sem,
-                device_id=(zs[w // 4] + y_at[w // 2 % 2], x_at[w % 2] + core_at), device_id_type=MESH,
-            ).start()
+        for dz in range(4):
+            row_to = zs[dz] + (y + dz + c + 1) % 4
+            for r in range(8):
+                if c is CHUNKS - 1 and dz == 0 and r == 0:
+                    continue
+                pltpu.make_async_remote_copy(
+                    send.at[c * GROUP + dz * 8 + r], recv.at[me], send_sem, recv_sem.at[c],
+                    device_id=(row_to, xs[r // 2] + cores[r % 2]), device_id_type=MESH,
+                ).start()
 
     def place_and_send(c, carry):
         place(c)
@@ -221,7 +217,7 @@
 
     lax.fori_loop(0, EARLY, place_and_send, 0)
     lax.fori_loop(EARLY, CHUNKS, place_only, 0)
-    own = pltpu.make_async_copy(send.at[SELF_GROUP * GROUP], recv.at[me], own_sem)
+    own = pltpu.make_async_copy(send.at[(CHUNKS - 1) * GROUP], recv.at[me], recv_sem.at[CHUNKS - 1])
     own.start()
 
     def all_of(ref, n, sem):
@@ -235,7 +231,7 @@
             sum1, stage2.at[serve_at], red_send.at[1], red_recv.at[1],
             device_id=(rows_at, xs[j // 2] + cores[j % 2]), device_id_type=MESH,
         ).start()
-    for c in range(EARLY, MIDDLE):
+    for c in range(EARLY, CHUNKS):
         send_group(c)
     stage2[serve_at] = sum1[...]
     all_of(stage2, N_SERVE - 1, red_recv.at[1])
@@ -245,24 +241,30 @@
             full.at[rows_at], full.at[rows_at], red_send.at[2], red_recv.at[2],
             device_id=(zs[j // 4] + ys[j % 4], serve_at), device_id_type=MESH,
         ).start()
-    for c in range(MIDDLE, CHUNKS):
-        send_group(c)
-    own.wait()
-    all_of(recv, DEVS - 1, recv_sem)
-    column = lax.broadcasted_iota(jnp.int32, (PART, LANES), 1)
-    for i in range(PARTS):
-        part = pl.ds(i * PART, PART)
-        packed = recv[i * PART // CAP:(i + 1) * PART // CAP].reshape(PART, LANES)
+    column = lax.broadcasted_iota(jnp.int32, (PLANE, LANES), 1)
+
+    def decode(n, carry):
+        c, dz = n // 4, n % 4
+        plane = (z + 4 - dz) % 4 * 4 + (y + 7 - dz - c) % 4
+
+        @pl.when(dz == 0)
+        def _():
+            all_of(recv, GROUP, recv_sem.at[c])
+
+        packed = recv[pl.ds(plane * 8, 8)].reshape(PLANE, LANES)
         b = (packed << 16) >> 16
         down = 1.0 / scale_up(b[:, 96:99].astype(F32))
         a = (packed >> 16).astype(F32) * down[:, 0:1]
         b = b.astype(F32) * jnp.where(column < 64, down[:, 1:2], jnp.where(column < 96, down[:, 2:3], 0.0))
+        at = pl.ds(pl.multiple_of(plane * PLANE, PLANE), PLANE)
         for k, rows in enumerate((a, b)):
             high, low = split(rows)
-            spread[k, part, :LANES] = high
-            spread[k, part, LANES:] = low
-    kept = pltpu.make_async_copy(spread, spread_hbm, out_sem)
-    kept.start()
+            spread[k, at, :LANES] = high
+            spread[k, at, LANES:] = low
+        pltpu.make_async_copy(spread.at[:, at], spread_hbm.at[:, at], out_sem).start()
+        return carry
+
+    lax.fori_loop(0, N_ROWS, decode, 0)
 
     all_of(full, N_ROWS - 1, red_recv.at[2])
 
@@ -285,7 +287,7 @@
         weights_ref[0:128, t * D:(t + 1) * D] = high
         weights_ref[128:256, t * D:(t + 1) * D] = low
 
-    kept.wait()
+    pltpu.make_async_copy(spread, spread_hbm, out_sem).wait()
     all_of(send, DEVS - 1, send_sem)
     all_of(stage1, N_ROWS - 1, red_send.at[0])
     all_of(stage2, N_SERVE - 1, red_send.at[1])
@@ -334,10 +336,9 @@
             pltpu.VMEM((N_ROWS, SHARE, 4, LANES), F32),
             pltpu.SemaphoreType.DMA((10,)),
             pltpu.SemaphoreType.DMA,
-            pltpu.SemaphoreType.DMA,
+            pltpu.SemaphoreType.DMA((CHUNKS,)),
             pltpu.SemaphoreType.DMA((3,)),
             pltpu.SemaphoreType.DMA((3,)),
-            pltpu.SemaphoreType.DMA,
             pltpu.SemaphoreType.DMA,
         ],
         compiler_params=pltpu.CompilerParams(

time: 35.9 us -> 33.4 us (0.930)
  Pallas kernels: 35.7 us -> 33.3 us
    pallas_call x1, Pallas kernels: 31.9 us -> 29.5 us  [local(): pl.pallas_call(front_kernel, out_shape=(jax.ShapeDtypeStruct((2, SLOTS, 2...]
where the time goes in v4:
time: 33.4 us; the launch traced here: 33.3 us
  Pallas kernels  33.3 us (100%)
    pallas_call x1, Pallas kernels, local(): pl.pallas_call(front_kernel, out_shape=(jax.ShapeDtypeStruct((2, SLOTS, 2...  29.5 us
    pallas_call x1, Pallas kernels, local(): pl.pallas_call(project_kernel, grid=(SLOTS // STRIPE,), out_shape=jax.Sha...  3.81 us

profile of v4, /device:TPU:1, one launch (start us, length us, event | category | flops | bytes accessed | tf_op | source)
XLA Modules:
  0.0 33.3 jit_solution(3689320309296104890)
XLA Ops:
  0.0 29.5 %step_and_route.1 = (bf16[2,1536,256]{2,1,0:T(8,128)(2,1)}, bf16[256,768]{1,0:T(8,128)(2,1)}) custom-call(f32[32,1024]{1,0:T(8,128)} %bitcast.5, f32[64,1024]{1,0:T(8,128)} %bitcast.4, f32[1024,128]{1,0:T(8,128)} %wide_hbm.1, f32[3,1024,256]{2,1,0:T(8,128)} %grads_hbm.1, f32[32,256]{1,0:T(8,128)} %ps_hbm.1, f32[64,256]{1,0:T(8,128)} %pm_hbm.1, ...), custom_call_target="tpu_custom_call" | custom-call | flops 4000000000 | bytes 8000000 | tf_op jit(solution)/shard_map/step_and_route/pallas_call | solution.py:307
  29.5 3.8 %project.1 = bf16[1536,768]{1,0:T(8,128)(2,1)} custom-call(bf16[2,1536,256]{2,1,0:T(8,128)(2,1)} %get-tuple-element.7.spread_ref, bf16[256,768]{1,0:T(8,128)(2,1)} %get-tuple-element.8.weights_ref), custom_call_target="tpu_custom_call" | custom-call | flops 1000000000 | bytes 5000000 | tf_op jit(solution)/shard_map/project/pallas_call | solution.py:353

commit v5 on v4

--- a/solution.py
+++ b/solution.py
@@ -10,6 +10,9 @@
 STEP_NORM = 16.0
 ROW_RATE = 0.1
 MESH = pl.DeviceIdType.MESH
+ALL_FAR_FIRST = sorted(
+    range(1, 128), key=lambda r: -sum(min(d, 4 - d) for d in (r // 32, r // 8 % 4, r // 2 % 4))
+)
 FAR_FIRST = sorted(range(1, 16), key=lambda j: -(min(j // 4, 4 - j // 4) + min(j % 4, 4 - j % 4)))
 N_ROWS = 16
 N_SERVE = 8
@@ -60,10 +63,10 @@
 
 def front_kernel(
     small_hbm, mid_hbm, wide_hbm, grads_hbm, ps_hbm, pm_hbm, pw_hbm, counts_ref, owners_hbm,
-    spread_hbm, weights_ref,
+    spread_hbm, weights_hbm,
     small, mid, wide, grads, ps, pm, pw, owners,
-    parts, placed_w, placed_m, placed_s, targets, send, recv, spread, totals, stage1, sum1, stage2, full,
-    in_sem, send_sem, recv_sem, red_send, red_recv, out_sem,
+    parts, placed_w, placed_m, placed_s, targets, send, recv, spread, weights_ref, totals, stage1, sum1, stage2, full,
+    in_sem, send_sem, recv_sem, red_send, red_recv, out_sem, w_sem,
 ):
     rows_at = lax.axis_index("rows")
     serve_at = lax.axis_index("serve")
@@ -84,7 +87,7 @@
         load.start()
 
     barrier = pltpu.get_barrier_semaphore()
-    for r in range(1, DEVS):
+    for r in ALL_FAR_FIRST:
         pl.semaphore_signal(
             barrier, inc=1, device_id_type=MESH,
             device_id=(zs[r // 32] + ys[r // 8 % 4], xs[r // 2 % 4] + cores[r % 2]),
@@ -264,7 +267,7 @@
         pltpu.make_async_copy(spread.at[:, at], spread_hbm.at[:, at], out_sem).start()
         return carry
 
-    lax.fori_loop(0, N_ROWS, decode, 0)
+    lax.fori_loop(0, 16, decode, 0)
 
     all_of(full, N_ROWS - 1, red_recv.at[2])
 
@@ -287,6 +290,9 @@
         weights_ref[0:128, t * D:(t + 1) * D] = high
         weights_ref[128:256, t * D:(t + 1) * D] = low
 
+    weights_out = pltpu.make_async_copy(weights_ref, weights_hbm, w_sem)
+    weights_out.start()
+    weights_out.wait()
     pltpu.make_async_copy(spread, spread_hbm, out_sem).wait()
     all_of(send, DEVS - 1, send_sem)
     all_of(stage1, N_ROWS - 1, red_send.at[0])
@@ -303,7 +309,6 @@
 
 def local(rows_small, rows_mid, rows_wide, row_grads, proj_small, proj_mid, proj_wide, counts, owners):
     hbm = pl.BlockSpec(memory_space=pl.ANY)
-    vmem = pl.BlockSpec(memory_space=pltpu.VMEM)
     spread, weights = pl.pallas_call(
         front_kernel,
         out_shape=(
@@ -311,7 +316,7 @@
             jax.ShapeDtypeStruct((2 * LANES, 3 * D), BF16),
         ),
         in_specs=[hbm] * 7 + [pl.BlockSpec(memory_space=pltpu.SMEM), hbm],
-        out_specs=(hbm, vmem),
+        out_specs=(hbm, hbm),
         scratch_shapes=[
             pltpu.VMEM((32, ROWS), F32),
             pltpu.VMEM((64, ROWS), F32),
@@ -329,6 +334,7 @@
             pltpu.VMEM((DEVS, 3, 4, LANES), jnp.int32),
             pltpu.VMEM((DEVS, 3, 4, LANES), jnp.int32),
             pltpu.VMEM((2, SLOTS, 2 * LANES), BF16),
+            pltpu.VMEM((2 * LANES, 3 * D), BF16),
             pltpu.VMEM((N_ROWS * SHARE, 4, LANES), F32),
             pltpu.VMEM((N_ROWS, SHARE, 4, LANES), F32),
             pltpu.VMEM((SHARE, 4, LANES), F32),
@@ -339,6 +345,7 @@
             pltpu.SemaphoreType.DMA((CHUNKS,)),
             pltpu.SemaphoreType.DMA((3,)),
             pltpu.SemaphoreType.DMA((3,)),
+            pltpu.SemaphoreType.DMA,
             pltpu.SemaphoreType.DMA,
         ],
         compiler_params=pltpu.CompilerParams(

time: 33.4 us -> 33.1 us (level)
  no operation moved by 1% of the time
where the time goes in v5:
time: 33.1 us; the launch traced here: 33 us
  Pallas kernels  33 us (100%)
    pallas_call x1, Pallas kernels, local(): pl.pallas_call(front_kernel, out_shape=(jax.ShapeDtypeStruct((2, SLOTS, 2...  29.2 us
    pallas_call x1, Pallas kernels, local(): pl.pallas_call(project_kernel, grid=(SLOTS // STRIPE,), out_shape=jax.Sha...  3.81 us

profile of v5, /device:TPU:1, one launch (start us, length us, event | category | flops | bytes accessed | tf_op | source)
XLA Modules:
  0.0 33.0 jit_solution(632489388351713536)
XLA Ops:
  0.0 29.2 %step_and_route.1 = (bf16[2,1536,256]{2,1,0:T(8,128)(2,1)}, bf16[256,768]{1,0:T(8,128)(2,1)}) custom-call(f32[32,1024]{1,0:T(8,128)} %bitcast.5, f32[64,1024]{1,0:T(8,128)} %bitcast.4, f32[1024,128]{1,0:T(8,128)} %wide_hbm.1, f32[3,1024,256]{2,1,0:T(8,128)} %grads_hbm.1, f32[32,256]{1,0:T(8,128)} %ps_hbm.1, f32[64,256]{1,0:T(8,128)} %pm_hbm.1, ...), custom_call_target="tpu_custom_call" | custom-call | flops 4000000000 | bytes 8000000 | tf_op jit(solution)/shard_map/step_and_route/pallas_call | solution.py:312
  29.2 3.8 %project.1 = bf16[1536,768]{1,0:T(8,128)(2,1)} custom-call(bf16[2,1536,256]{2,1,0:T(8,128)(2,1)} %get-tuple-element.7.spread_ref, bf16[256,768]{1,0:T(8,128)(2,1)} %get-tuple-element.8.weights_ref), custom_call_target="tpu_custom_call" | custom-call | flops 1000000000 | bytes 5000000 | tf_op jit(solution)/shard_map/project/pallas_call | solution.py:360

commit v6 on v5

--- a/solution.py
+++ b/solution.py
@@ -27,6 +27,7 @@
 CHUNKS = DEVS // GROUP
 SHARE = 7
 FINE = 64
+SELF_GROUP = 2
 EARLY = 2
 STRIPE = 768
 PLANE = 8 * CAP
@@ -136,7 +137,8 @@
         owner = owners[t]
         dz, dy = ((owner >> 5) - z) & 3, ((owner >> 3) - y) & 3
         dx, dc = ((owner >> 1) - x) & 3, (owner - core) & 1
-        chunk = (dy - dz - 1) & 3
+        apart = (dy - dz) & 3
+        chunk = jnp.where((apart & 1) == 1, apart >> 1, 2 + (apart >> 1))
         block = chunk * GROUP + dz * 8 + dx * 2 + dc
         live = lane < counts_ref[0, t]
         targets[t] = jnp.where(live, block * CAP + rank[t:t + 1], -1)
@@ -198,11 +200,14 @@
         packed = (a.astype(jnp.int32) << 16) | (b.astype(jnp.int32) & 0xFFFF)
         send[pl.ds(c * GROUP, GROUP)] = packed.reshape(GROUP, 3, 4, LANES)
 
+    def apart_of(c):
+        return jnp.where(c < 2, 1 + 2 * c, 2 * c - 4)
+
     def send_group(c):
-        for dz in range(4):
-            row_to = zs[dz] + (y + dz + c + 1) % 4
-            for r in range(8):
-                if c is CHUNKS - 1 and dz == 0 and r == 0:
+        for dz in (2, 1, 3, 0):
+            row_to = zs[dz] + (y + dz + apart_of(c)) % 4
+            for r in (4, 5, 2, 3, 6, 7, 0, 1):
+                if c is SELF_GROUP and dz == 0 and r == 0:
                     continue
                 pltpu.make_async_remote_copy(
                     send.at[c * GROUP + dz * 8 + r], recv.at[me], send_sem, recv_sem.at[c],
@@ -220,7 +225,7 @@
 
     lax.fori_loop(0, EARLY, place_and_send, 0)
     lax.fori_loop(EARLY, CHUNKS, place_only, 0)
-    own = pltpu.make_async_copy(send.at[(CHUNKS - 1) * GROUP], recv.at[me], recv_sem.at[CHUNKS - 1])
+    own = pltpu.make_async_copy(send.at[SELF_GROUP * GROUP], recv.at[me], recv_sem.at[SELF_GROUP])
     own.start()
 
     def all_of(ref, n, sem):
@@ -246,13 +251,8 @@
         ).start()
     column = lax.broadcasted_iota(jnp.int32, (PLANE, LANES), 1)
 
-    def decode(n, carry):
-        c, dz = n // 4, n % 4
-        plane = (z + 4 - dz) % 4 * 4 + (y + 7 - dz - c) % 4
-
-        @pl.when(dz == 0)
-        def _():
-            all_of(recv, GROUP, recv_sem.at[c])
+    def decode(c, dz):
+        plane = (z + 4 - dz) % 4 * 4 + (y + 8 - dz - apart_of(c)) % 4
 
         packed = recv[pl.ds(plane * 8, 8)].reshape(PLANE, LANES)
         b = (packed << 16) >> 16
@@ -265,9 +265,14 @@
             spread[k, at, :LANES] = high
             spread[k, at, LANES:] = low
         pltpu.make_async_copy(spread.at[:, at], spread_hbm.at[:, at], out_sem).start()
+
+    def decode_group(c, carry):
+        all_of(recv, GROUP, recv_sem.at[c])
+        for dz in range(4):
+            decode(c, dz)
         return carry
 
-    lax.fori_loop(0, 16, decode, 0)
+    lax.fori_loop(0, CHUNKS, decode_group, 0)
 
     all_of(full, N_ROWS - 1, red_recv.at[2])
 

time: 33.1 us -> 32.9 us (level)
  no operation moved by 1% of the time
where the time goes in v6:
time: 32.9 us; the launch traced here: 32.8 us
  Pallas kernels  32.8 us (100%)
    pallas_call x1, Pallas kernels, local(): pl.pallas_call(front_kernel, out_shape=(jax.ShapeDtypeStruct((2, SLOTS, 2...  29 us
    pallas_call x1, Pallas kernels, local(): pl.pallas_call(project_kernel, grid=(SLOTS // STRIPE,), out_shape=jax.Sha...  3.81 us

profile of v6, /device:TPU:1, one launch (start us, length us, event | category | flops | bytes accessed | tf_op | source)
XLA Modules:
  0.0 32.8 jit_solution(2131517015658903763)
XLA Ops:
  0.0 29.0 %step_and_route.1 = (bf16[2,1536,256]{2,1,0:T(8,128)(2,1)}, bf16[256,768]{1,0:T(8,128)(2,1)}) custom-call(f32[32,1024]{1,0:T(8,128)} %bitcast.5, f32[64,1024]{1,0:T(8,128)} %bitcast.4, f32[1024,128]{1,0:T(8,128)} %wide_hbm.1, f32[3,1024,256]{2,1,0:T(8,128)} %grads_hbm.1, f32[32,256]{1,0:T(8,128)} %ps_hbm.1, f32[64,256]{1,0:T(8,128)} %pm_hbm.1, ...), custom_call_target="tpu_custom_call" | custom-call | flops 4000000000 | bytes 8000000 | tf_op jit(solution)/shard_map/step_and_route/pallas_call | solution.py:317
  29.0 3.8 %project.1 = bf16[1536,768]{1,0:T(8,128)(2,1)} custom-call(bf16[2,1536,256]{2,1,0:T(8,128)(2,1)} %get-tuple-element.7.spread_ref, bf16[256,768]{1,0:T(8,128)(2,1)} %get-tuple-element.8.weights_ref), custom_call_target="tpu_custom_call" | custom-call | flops 1000000000 | bytes 5000000 | tf_op jit(solution)/shard_map/project/pallas_call | solution.py:365

commit v7 on v6

--- a/solution.py
+++ b/solution.py
@@ -84,15 +84,17 @@
     grad_loads = [
         pltpu.make_async_copy(grads_hbm.at[t], grads.at[t], in_sem.at[len(loads) + t]) for t in range(3)
     ]
-    for load in (loads[3], grad_loads[2], loads[2], grad_loads[1], loads[1], grad_loads[0], *loads[4:], loads[0]):
-        load.start()
-
+    loads[3].start()
+    grad_loads[2].start()
     barrier = pltpu.get_barrier_semaphore()
     for r in ALL_FAR_FIRST:
         pl.semaphore_signal(
             barrier, inc=1, device_id_type=MESH,
             device_id=(zs[r // 32] + ys[r // 8 % 4], xs[r // 2 % 4] + cores[r % 2]),
         )
+
+    for load in (loads[2], grad_loads[1], loads[1], grad_loads[0], *loads[4:], loads[0]):
+        load.start()
 
     at = 0
     row = lax.broadcasted_iota(jnp.int32, (ROWS, D), 0)

time: 32.9 us -> 33.1 us (level)
  no operation moved by 1% of the time
where the time goes in v7:
time: 33.1 us; the launch traced here: 32.9 us
  Pallas kernels  32.9 us (99%)
    pallas_call x1, Pallas kernels, local(): pl.pallas_call(front_kernel, out_shape=(jax.ShapeDtypeStruct((2, SLOTS, 2...  29.1 us
    pallas_call x1, Pallas kernels, local(): pl.pallas_call(project_kernel, grid=(SLOTS // STRIPE,), out_shape=jax.Sha...  3.81 us

profile of v7, /device:TPU:1, one launch (start us, length us, event | category | flops | bytes accessed | tf_op | source)
XLA Modules:
  0.0 32.9 jit_solution(2336918698397502515)
XLA Ops:
  0.0 29.1 %step_and_route.1 = (bf16[2,1536,256]{2,1,0:T(8,128)(2,1)}, bf16[256,768]{1,0:T(8,128)(2,1)}) custom-call(f32[32,1024]{1,0:T(8,128)} %bitcast.5, f32[64,1024]{1,0:T(8,128)} %bitcast.4, f32[1024,128]{1,0:T(8,128)} %wide_hbm.1, f32[3,1024,256]{2,1,0:T(8,128)} %grads_hbm.1, f32[32,256]{1,0:T(8,128)} %ps_hbm.1, f32[64,256]{1,0:T(8,128)} %pm_hbm.1, ...), custom_call_target="tpu_custom_call" | custom-call | flops 4000000000 | bytes 8000000 | tf_op jit(solution)/shard_map/step_and_route/pallas_call | solution.py:319
  29.1 3.8 %project.1 = bf16[1536,768]{1,0:T(8,128)(2,1)} custom-call(bf16[2,1536,256]{2,1,0:T(8,128)(2,1)} %get-tuple-element.7.spread_ref, bf16[256,768]{1,0:T(8,128)(2,1)} %get-tuple-element.8.weights_ref), custom_call_target="tpu_custom_call" | custom-call | flops 1000000000 | bytes 5000000 | tf_op jit(solution)/shard_map/project/pallas_call | solution.py:367
